TPU v7x, 512 devices: a whole 4x4x16 slice. The times are simulated.
512 devices in a mesh: section: 4 (over x), seq: 16 (over z), tp: 8 (over y, core).
Axes of the slice: x: 4, y: 4, z: 16, core: 2. Of those that a mesh axis runs over, the one named last changes fastest.
Arguments:
- merged_hidden: bfloat16 [3072, 5120], P('section', 'seq'), may hold values from -6 to 6
- merger_weight: bfloat16 [5120, 8192], P('seq', 'tp'), may hold values from -0.078125 to 0.078125
- merger_bias: float32 [8192], P('tp'), may hold values from -3 to 3
- text_embed: bfloat16 [16384, 8192], P(('section', 'seq'), 'tp'), may hold values from -108 to 108
- image_tokens: int32 [64, 4], P(('section', 'seq')), may hold values from 1 to 45, as said below
- image_offsets: int32 [64, 4], P(('section', 'seq')), may hold values from 1 to 191, as said below
- prefill_gain: bfloat16 [8192], P('tp'), may hold values from 0.099609375 to 1.8984375
- kv_weight: bfloat16 [8192, 2048], P('seq', 'tp'), may hold values from -0.0625 to 0.0625
- kv_bias: float32 [2048], P('tp'), may hold values from -4 to 4
- prompt_lengths: int32 [64], replicated, may hold values from 193 to 256, as said below
- queries: bfloat16 [1024, 8192], P(('section', 'seq'), 'tp'), may hold values from -5 to 5
- cache_pages: bfloat16 [15360, 16, 2048], P(('section', 'seq'), None, 'tp'), may hold values from -5 to 5
- page_tables: int32 [960, 16], P(('section', 'seq')), may hold values from 0 to 239, as said below
- context_lengths: int32 [960], P(('section', 'seq')), may hold values from 2 to 256, as said below
Outputs:
- prompt_cache: bfloat16 [16384, 2048], P(('section', 'seq'), 'tp')
- decode_out: bfloat16 [1024, 8192], P(('section', 'seq'), 'tp')
Inputs may be any that keep to these rules, and one draw needn't show every extreme that they name: `image_tokens`: each prompt's image token counts sum to 48. `image_offsets`: images of a prompt lie in order and apart, within its first 192 positions. `prompt_lengths`: some prompt has 256 tokens; every image of a prompt ends before its length. `context_lengths`: some request has 256 cached positions. `page_tables`: the pages of one owner's resident requests are distinct pages of that owner's block.
All inputs are finite; a program needn't handle non-finite values.
Results may differ from a plain program's by a relative error of at most 0.0047.
Values may be sent and summed in bfloat16 or wider, within the bound.
No kernel may reach another device: no remote copies, remote signals or barrier semaphores. Data moves between devices by JAX's collectives and lax.ppermute only.
A program may use at most 64 MiB of HBM per device.

v0:
```python
import math

import jax
import jax.numpy as jnp
from jax import lax
from jax.sharding import PartitionSpec as P

D = 8192
HD = 128


EPSILON = 1e-06
THETA = 1000000.0
MASKED = -1e30


def passed_along(value, axis, steps):
    count = lax.axis_size(axis)
    pairs = [(source, (source + steps) % count) for source in range(count)]
    return lax.ppermute(value, axis, pairs)


def place_images(text_rows, image_rows, image_counts, image_starts):
    positions = jnp.arange(text_rows.shape[0], dtype=jnp.int32)[:, None]
    earlier = jnp.cumsum(image_counts) - image_counts
    inside_img = (positions >= image_starts[None, :]) & (
        positions < (image_starts + image_counts)[None, :]
    )
    source_row = jnp.sum(
        jnp.where(inside_img, earlier[None, :] + positions - image_starts[None, :], 0), axis=1
    )
    covered = jnp.any(inside_img, axis=1)
    picked_rows = jnp.take(image_rows, source_row, axis=0)
    return jnp.where(covered[:, None], picked_rows, text_rows)


def rotate_keys(packed, head_dim):
    seq_len = packed.shape[0]
    head_count = packed.shape[1] // (2 * head_dim)
    head_grid = packed.reshape(seq_len, head_count, 2, head_dim)
    key_part = head_grid[:, :, 0, :]
    value_part = head_grid[:, :, 1, :]
    half_dim = head_dim // 2
    frequency = THETA ** (-jnp.arange(half_dim, dtype=jnp.float32) * 2.0 / head_dim)
    angles = jnp.arange(seq_len, dtype=jnp.float32)[:, None] * frequency[None, :]
    cosine = jnp.cos(angles)[:, None, :]
    sine_table = jnp.sin(angles)[:, None, :]
    first_half = key_part[..., :half_dim]
    second_half = key_part[..., half_dim:]
    rotated = jnp.concatenate(
        [
            first_half * cosine - second_half * sine_table,
            second_half * cosine + first_half * sine_table,
        ],
        axis=-1,
    )
    return (
        jnp.stack([rotated, value_part], axis=2)
        .reshape(seq_len, head_count * 2 * head_dim)
        .astype(jnp.bfloat16)
    )


def attend(asked, page_pool, page_table, live_lengths, head_dim):
    request_count = asked.shape[0]
    head_count = page_pool.shape[2] // (2 * head_dim)
    per_head = asked.shape[1] // (head_count * head_dim)
    gathered = jnp.take(page_pool, page_table, axis=0)
    context_span = page_table.shape[1] * page_pool.shape[1]
    gathered = gathered.reshape(request_count, context_span, head_count, 2, head_dim)
    key_rows = gathered[:, :, :, 0, :]
    value_rows = gathered[:, :, :, 1, :]
    grouped = asked.reshape(request_count, head_count, per_head, head_dim)
    scores = jnp.einsum(
        "rhgd,rthd->rhgt", grouped, key_rows, preferred_element_type=jnp.float32
    ) / math.sqrt(head_dim)
    live_mask = jnp.arange(context_span, dtype=jnp.int32)[None, :] < live_lengths[:, None]
    scores = jnp.where(live_mask[:, None, None, :], scores, MASKED)
    row_max = jnp.max(scores, axis=-1, keepdims=True)
    weights = jnp.exp(scores - row_max)
    weights = (weights / jnp.sum(weights, axis=-1, keepdims=True)).astype(jnp.bfloat16)
    mixed = jnp.einsum("rhgt,rthd->rhgd", weights, value_rows, preferred_element_type=jnp.float32)
    return mixed.reshape(request_count, head_count * per_head * head_dim).astype(jnp.bfloat16)


def per_device(
    merged_hidden,
    merger_weight,
    merger_bias,
    text_embed,
    image_tokens,
    image_offsets,
    prefill_gain,
    kv_weight,
    kv_bias,
    prompt_lengths,
    queries,
    cache_pages,
    page_tables,
    context_lengths,
):
    summed = lax.psum_scatter(
        jnp.dot(merged_hidden, merger_weight, preferred_element_type=jnp.float32),
        "seq",
        scatter_dimension=0,
        tiled=True,
    )
    image_rows = (summed + merger_bias).astype(jnp.bfloat16)
    arrived = passed_along(image_rows, "section", 1)
    embedded = place_images(text_embed, arrived, image_tokens[0], image_offsets[0])
    widened = embedded.astype(jnp.float32)
    squares = lax.psum(jnp.sum(widened * widened, axis=1), "tp")
    scaling = lax.rsqrt(squares / D + EPSILON)[:, None]
    normed_part = (widened * scaling * prefill_gain.astype(jnp.float32)).astype(jnp.bfloat16)
    normed_all = lax.all_gather(normed_part, "tp", axis=1, tiled=True)
    projected = (
        jnp.dot(
            normed_all,
            lax.all_gather(kv_weight, "seq", axis=0, tiled=True),
            preferred_element_type=jnp.float32,
        )
        + kv_bias
    )
    prompt_cache = rotate_keys(projected, HD)
    fresh_rows = passed_along(prompt_cache, "section", 1)
    section_count = lax.axis_size("section")
    previous = (lax.axis_index("section") + section_count - 1) % section_count * lax.axis_size(
        "seq"
    ) + lax.axis_index("seq")
    fresh_length = lax.dynamic_slice_in_dim(prompt_lengths, previous, 1, 0)
    page_rows = cache_pages.shape[1]
    pages_each = page_tables.shape[1]
    fresh_pages = fresh_rows.reshape(pages_each, page_rows, fresh_rows.shape[1])
    combined = jnp.concatenate([cache_pages, fresh_pages], axis=0)
    appended = (cache_pages.shape[0] + jnp.arange(pages_each, dtype=jnp.int32))[None, :]
    all_tables = jnp.concatenate([page_tables, appended], axis=0)
    all_lengths = jnp.concatenate([context_lengths, fresh_length], axis=0)
    decode_out = attend(queries, combined, all_tables, all_lengths, HD)
    return (prompt_cache, decode_out)


def solution(mesh):
    return jax.shard_map(
        per_device,
        mesh=mesh,
        in_specs=(
            P("section", "seq"),
            P("seq", "tp"),
            P("tp"),
            P(("section", "seq"), "tp"),
            P(("section", "seq"), None),
            P(("section", "seq"), None),
            P("tp"),
            P("seq", "tp"),
            P("tp"),
            P(),
            P(("section", "seq"), "tp"),
            P(("section", "seq"), None, "tp"),
            P(("section", "seq"), None),
            P(("section", "seq")),
        ),
        out_specs=(P(("section", "seq"), "tp"), P(("section", "seq"), "tp")),
        check_vma=False,
    )
```

profile of v0, /device:TPU:1, one launch (start us, length us, event | category | flops | bytes accessed | tf_op | source)
XLA Modules:
  0.0 243.0 jit_solution(7805435532684427772)
XLA Ops:
  7.2 1.0 copy-done
  8.3 3.7 %fusion.15 = f32[768,1024]{1,0:T(8,128)} fusion(bf16[768,320]{0,1:T(8,128)(2,1)} %param.14, bf16[320,1024]{1,0:T(8,128)(2,1)S(1)} %copy-done), kind=kOutput, calls=%fused_computation.55 | convolution fusion | flops 503316480 | bytes 4292608 | tf_op jit(solution)/shard_map/dot_general | solution.py:103
  12.1 0.7 all-gather.5.cloned.1.call-update
  12.8 0.2 reduce-window_clone.1
  13.2 71.5 %reduce-scatter.2.cloned.1.call-done = f32[48,1024]{1,0:T(8,128)} async-done(((f32[768,1024]{1,0:T(8,128)}), f32[48,1024]{1,0:T(8,128)}) %reduce-scatter.2.cloned.1.call-update) | async-done | bytes 196624 | tf_op jit(solution)/shard_map/reduce_scatter | solution.py:102
  84.7 0.9 add_convert_fusion
  85.7 3.3 %collective-permute-start = (bf16[48,1024]{1,0:T(8,128)(2,1)S(1)}, bf16[48,1024]{1,0:T(8,128)(2,1)S(1)}, u32[]{:S(2)}, u32[]{:S(2)}) collective-permute-start(bf16[48,1024]{1,0:T(8,128)(2,1)S(1)} %add_convert_fusion), channel_id=1, source_target_pairs={{0,128},{128,256},{256,384},{384,0},{1,129},{129,257},{257,385},{3... | collective-permute-start | bytes 294920 | tf_op jit(solution)/shard_map/ppermute | solution.py:20
  89.0 3.3 %collective-permute-done = bf16[48,1024]{1,0:T(8,128)(2,1)S(1)} collective-permute-done((bf16[48,1024]{1,0:T(8,128)(2,1)S(1)}, bf16[48,1024]{1,0:T(8,128)(2,1)S(1)}, u32[]{:S(2)}, u32[]{:S(2)}) %collective-permute-start) | collective-permute-done | bytes 98336 | tf_op jit(solution)/shard_map/ppermute | solution.py:20
  92.4 1.2 gather_fusion
  93.6 0.4 fusion.5
  94.0 22.9 %psum.7 = f32[256]{0:T(256)S(1)} all-reduce(f32[256]{0:T(256)S(1)} %get-tuple-element.2), channel_id=1, replica_groups=mesh['section'=4,'seq'=16,'tp'=8] {'tp'}, use_global_device_ids=true, to_apply=%region_5.6 | all-reduce | flops 256 | bytes 2048 | tf_op jit(solution)/shard_map/psum | solution.py:112
  116.9 1.0 fusion.7
  118.0 0.6 dynamic_slice.3
  118.6 0.7 pad_add_fusion
  119.4 44.5 %all-gather.5.cloned.1.call-done = bf16[8192,256]{1,0:T(8,128)(2,1)} async-done(((bf16[512,256]{1,0:T(8,128)(2,1)}), bf16[8192,256]{1,0:T(8,128)(2,1)}) %all-gather.5.cloned.1.call-update) | async-done | bytes 4194320 | tf_op jit(solution)/shard_map/all_gather | solution.py:119
  163.9 47.5 %all-gather.3.cloned.1.call-done = bf16[256,8192]{1,0:T(8,128)(2,1)} async-done(((bf16[256,1024]{1,0:T(8,128)(2,1)}), bf16[256,8192]{1,0:T(8,128)(2,1)}) %all-gather.3.cloned.1.call-update) | async-done | bytes 4194320 | tf_op jit(solution)/shard_map/all_gather | solution.py:115
  211.4 5.2 %convolution_add_fusion = f32[256,256]{0,1:T(8,128)S(1)} fusion(bf16[256,8192]{1,0:T(8,128)(2,1)} %all-gather.3.cloned.1.call-done, bf16[8192,256]{1,0:T(8,128)(2,1)} %all-gather.5.cloned.1.call-done, f32[256]{0:T(256)S(1)} %copy-done.7), kind=kOutput, calls=%fused_computation.7 | convolution fusion | flops 1073807360 | bytes 8651776 | tf_op jit(solution)/shard_map/dot_general | solution.py:117
  216.7 0.3 subtract_convert_fusion
  217.1 0.1 copy.24
  217.2 3.1 %collective-permute-start.1 = (bf16[256,256]{1,0:T(8,128)(2,1)S(1)}, bf16[256,256]{1,0:T(8,128)(2,1)S(1)}, u32[]{:S(2)}, u32[]{:S(2)}) collective-permute-start(bf16[256,256]{1,0:T(8,128)(2,1)S(1)} %copy.24), channel_id=1, source_target_pairs={{0,128},{128,256},{256,384},{384,0},{1,129},{129,257},{257,385},{3... | collective-permute-start | bytes 393224 | tf_op jit(solution)/shard_map/ppermute | solution.py:20
  220.4 0.1 broadcast_in_dim.71
  220.5 0.1 broadcast_in_dim.72
  220.6 4.5 %collective-permute-done.1 = bf16[256,256]{1,0:T(8,128)(2,1)S(1)} collective-permute-done((bf16[256,256]{1,0:T(8,128)(2,1)S(1)}, bf16[256,256]{1,0:T(8,128)(2,1)S(1)}, u32[]{:S(2)}, u32[]{:S(2)}) %collective-permute-start.1) | collective-permute-done | bytes 131104 | tf_op jit(solution)/shard_map/ppermute | solution.py:20
  225.1 1.7 pad_maximum_fusion
  226.9 2.1 gather_fusion.1
  229.0 2.5 %gather.12 = bf16[16,256,1,2,128]{4,3,1,0,2:T(2,128)(2,1)S(1)} reshape(bf16[256,16,256]{2,1,0:T(8,128)(2,1)} %gather_fusion.1) | data formatting | bytes 4194304 | tf_op jit(solution)/shard_map/jit(_take)/gather | solution.py:68
  231.5 0.9 copy_select_fusion
  232.4 1.3 copy-done.1
  233.8 0.4 fusion.4
  234.2 0.2 fusion.14
  234.3 1.5 convolution_convert_fusion
  235.9 0.6 copy.29
  (50 shorter events, 0.7 us)
Async XLA Ops:
  7.2 1.1 copy-start
  7.2 77.6 %reduce-scatter.2.cloned.1.call-start = ((), (), s32[]{:S(2)}) async-start(), calls=%async_computation.1 | async-start | bytes 3342336 | tf_op jit(solution)/shard_map/reduce_scatter | solution.py:102
  12.0 0.8 copy-start.8
  12.0 0.9 copy-start.10
  12.0 1.0 copy-start.9
  12.0 72.8 %copy-start.6 = (f32[1024]{0:T(1024)S(1)}, f32[1024]{0:T(1024)}, u32[]{:S(2)}) copy-start(f32[1024]{0:T(1024)} %param.16) | copy-start | bytes 12292
  12.0 151.9 %all-gather.5.cloned.1.call-start = ((), (), s32[]{:S(2)}) async-start(), calls=%async_computation.3 | async-start | bytes 4456448 | tf_op jit(solution)/shard_map/all_gather | solution.py:119
  12.8 198.6 %all-gather.3.cloned.1.call-start = ((), (), s32[]{:S(2)}) async-start(), calls=%async_computation.2 | async-start | bytes 4718592 | tf_op jit(solution)/shard_map/all_gather | solution.py:115
  85.7 6.7 %collective-permute-start = (bf16[48,1024]{1,0:T(8,128)(2,1)S(1)}, bf16[48,1024]{1,0:T(8,128)(2,1)S(1)}, u32[]{:S(2)}, u32[]{:S(2)}) collective-permute-start(bf16[48,1024]{1,0:T(8,128)(2,1)S(1)} %add_convert_fusion), channel_id=1, source_target_pairs={{0,128},{128,256},{256,384},{384,0},{1,129},{129,257},{257,385},{3... | collective-permute-start | bytes 294920 | tf_op jit(solution)/shard_map/ppermute | solution.py:20
  89.0 4.5 %copy-start.2 = (bf16[256,1024]{1,0:T(8,128)(2,1)S(1)}, bf16[256,1024]{1,0:T(8,128)(2,1)}, u32[]{:S(2)}) copy-start(bf16[256,1024]{1,0:T(8,128)(2,1)} %param.17) | copy-start | bytes 1572868
  93.5 24.4 %copy-start.11 = (s32[64]{0:T(128)S(1)}, s32[64]{0:T(128)}, u32[]{:S(2)}) copy-start(s32[64]{0:T(128)} %param.23) | copy-start | bytes 772
  93.6 25.0 %copy-start.12 = (s32[15]{0:T(128)S(1)}, s32[15]{0:T(128)}, u32[]{:S(2)}) copy-start(s32[15]{0:T(128)} %param.27) | copy-start | bytes 184
  93.6 25.7 %copy-start.5 = (s32[15,16]{1,0:T(8,128)S(1)}, s32[15,16]{1,0:T(8,128)}, u32[]{:S(2)}) copy-start(s32[15,16]{1,0:T(8,128)} %param.26) | copy-start | bytes 2884
  93.6 117.8 %copy-start.7 = (f32[256]{0:T(256)S(1)}, f32[256]{0:T(256)}, u32[]{:S(2)}) copy-start(f32[256]{0:T(256)} %param.22) | copy-start | bytes 3076
  119.4 101.2 %copy-start.4 = (bf16[16,1024]{1,0:T(8,128)(2,1)S(1)}, bf16[16,1024]{1,0:T(8,128)(2,1)}, u32[]{:S(2)}) copy-start(bf16[16,1024]{1,0:T(8,128)(2,1)} %param.24) | copy-start | bytes 98308
  217.2 9.7 %copy-start.3 = (bf16[256,256]{1,0:T(8,128)(2,1)}, bf16[256,256]{1,0:T(8,128)(2,1)S(1)}, u32[]{:S(2)}) copy-start(bf16[256,256]{1,0:T(8,128)(2,1)S(1)} %copy.24) | copy-start | bytes 393220
  217.2 7.9 %collective-permute-start.1 = (bf16[256,256]{1,0:T(8,128)(2,1)S(1)}, bf16[256,256]{1,0:T(8,128)(2,1)S(1)}, u32[]{:S(2)}, u32[]{:S(2)}) collective-permute-start(bf16[256,256]{1,0:T(8,128)(2,1)S(1)} %copy.24), channel_id=1, source_target_pairs={{0,128},{128,256},{256,384},{384,0},{1,129},{129,257},{257,385},{3... | collective-permute-start | bytes 393224 | tf_op jit(solution)/shard_map/ppermute | solution.py:20
  232.4 1.3 copy-start.1
Sparse Core Ops, SparseCore 0:
  12.1 72.5 reduce-scatter.1
  86.8 77.0 all-gather.4
  166.0 45.3 all-gather.2
where the time goes:
time: 243 us
  waiting for transfers between devices  172 us (71%)
  blocking collectives  22.9 us (9%)
  between operations  14 us (6%)
  matrix products  10.9 us (4%)
  local copies, waits for them, and re-layouts  9.9 us (4%)
  other arithmetic  6.76 us (3%)
  starting transfers between devices  6.55 us (3%)
    reduce_scatter x1, waiting for transfers between devices, per_device(): lax.psum_scatter(jnp.dot(merged_hidden, merger_weight, preferred_element_...  71.5 us
    all_gather x1, waiting for transfers between devices, per_device(): normed_all = lax.all_gather(normed_part, 'tp', axis=1, tiled=True)  47.5 us
    all_gather x1, waiting for transfers between devices, per_device(): lax.all_gather(kv_weight, 'seq', axis=0, tiled=True)  44.5 us
    psum x1, blocking collectives, per_device(): squares = lax.psum(jnp.sum(widened * widened, axis=1), 'tp')  22.9 us
    ppermute x2, waiting for transfers between devices, passed_along(): return lax.ppermute(value, axis, pairs)  7.79 us
    ppermute x2, starting transfers between devices, passed_along(): return lax.ppermute(value, axis, pairs)  6.43 us
    dot_general x1, matrix products, per_device(): jnp.dot(normed_all, lax.all_gather(kv_weight, 'seq', axis=0, tiled=True),...  5.24 us
  transfers between devices with their start and end apart: 5, of which 5 were waited for; matrix products, arithmetic and copies ran while one was open for 2% of the time, Pallas kernels for 0%

commit v1 on v0

--- a/solution.py
+++ b/solution.py
@@ -14,13 +14,89 @@
 MASKED = -1e30
 
 
-def passed_along(value, axis, steps):
-    count = lax.axis_size(axis)
-    pairs = [(source, (source + steps) % count) for source in range(count)]
-    return lax.ppermute(value, axis, pairs)
-
-
-def place_images(text_rows, image_rows, image_counts, image_starts):
+def hop(value, section_steps, seq_steps):
+    sections = lax.axis_size("section")
+    owners = lax.axis_size("seq")
+    pairs = [
+        (x * owners + z, (x + section_steps) % sections * owners + (z + seq_steps) % owners)
+        for x in range(sections)
+        for z in range(owners)
+    ]
+    return lax.ppermute(value, ("section", "seq"), pairs)
+
+
+def tp_hop(value, steps):
+    count = lax.axis_size("tp")
+    return lax.ppermute(value, "tp", [(t, (t + steps) % count) for t in range(count)])
+
+
+def core_swap(value):
+    return lax.ppermute(value, "tp", [(t, t ^ 1) for t in range(lax.axis_size("tp"))])
+
+
+def merged_images(merged_hidden, merger_weight, merger_bias):
+    f32 = jnp.float32
+    z = lax.axis_index("seq")
+    blocks = merged_hidden.reshape(4, 4, 48, merged_hidden.shape[1])
+
+    def share(step):
+        rows = lax.dynamic_index_in_dim(blocks, (z + step) % 4, axis=1, keepdims=False)
+        return jnp.dot(
+            rows.reshape(192, rows.shape[2]), merger_weight, preferred_element_type=f32
+        )
+
+    half = merger_weight.shape[1] // 2
+    far = share(2).astype(jnp.bfloat16)
+    far_low = hop(far[:, :half], 0, 2)
+    far_high = hop(far[:, half:], 0, -2)
+    right = hop(share(1).astype(jnp.bfloat16), 0, 1)
+    left = hop(share(3).astype(jnp.bfloat16), 0, -1)
+    own = share(0)
+    total = (
+        own
+        + right.astype(f32)
+        + left.astype(f32)
+        + jnp.concatenate([far_low, far_high], axis=1).astype(f32)
+    )
+    total = total.astype(jnp.bfloat16).reshape(4, 48, total.shape[1])
+
+    def block(step):
+        return lax.dynamic_index_in_dim(total, (z // 4 + step) % 4, axis=0, keepdims=False)
+
+    summed = merger_bias
+    for step in (2, 1, 3, 0):
+        summed = summed + hop(block(step), 1, 4 * step).astype(f32)
+    return summed.astype(jnp.bfloat16)
+
+
+def gathered_text(text_embed, gain):
+    t = lax.axis_index("tp")
+    y, core = t // 2, t % 2
+    rows = text_embed.shape[0]
+    sent = jnp.concatenate(
+        [text_embed, jnp.broadcast_to(gain[None, :], (16, gain.shape[0]))], axis=0
+    )
+    mine = jnp.stack([sent, tp_hop(sent, -2), tp_hop(sent, 4), tp_hop(sent, 2)])
+    others = core_swap(mine)
+    both = jnp.stack([mine, others])
+    parts = []
+    for k in range(lax.axis_size("tp")):
+        part = lax.dynamic_slice(
+            both, ((core + k) % 2, (k // 2 - y) % 4, 0, 0), (1, 1) + sent.shape
+        )
+        parts.append(part.reshape(sent.shape))
+    whole = jnp.concatenate(parts, axis=1)
+    return whole[:rows], whole[rows]
+
+
+def normalized(rows, gain):
+    widened = rows.astype(jnp.float32)
+    squares = jnp.sum(widened * widened, axis=1, keepdims=True)
+    scaling = lax.rsqrt(squares / D + EPSILON)
+    return (widened * scaling * gain.astype(jnp.float32)).astype(jnp.bfloat16)
+
+
+def placed(text_rows, image_rows, image_counts, image_starts):
     positions = jnp.arange(text_rows.shape[0], dtype=jnp.int32)[:, None]
     earlier = jnp.cumsum(image_counts) - image_counts
     inside_img = (positions >= image_starts[None, :]) & (
@@ -83,6 +159,19 @@
     return mixed.reshape(request_count, head_count * per_head * head_dim).astype(jnp.bfloat16)
 
 
+def attend_fresh(asked, prompt_cache, length, head_dim):
+    keys = prompt_cache[:, :head_dim]
+    values = prompt_cache[:, head_dim:]
+    scores = jnp.einsum("gd,td->gt", asked, keys, preferred_element_type=jnp.float32)
+    scores = scores / math.sqrt(head_dim)
+    live = jnp.arange(keys.shape[0], dtype=jnp.int32)[None, :] < length
+    scores = jnp.where(live, scores, MASKED)
+    weights = jnp.exp(scores - jnp.max(scores, axis=-1, keepdims=True))
+    weights = (weights / jnp.sum(weights, axis=-1, keepdims=True)).astype(jnp.bfloat16)
+    mixed = jnp.einsum("gt,td->gd", weights, values, preferred_element_type=jnp.float32)
+    return mixed.astype(jnp.bfloat16)
+
+
 def per_device(
     merged_hidden,
     merger_weight,
@@ -99,43 +188,23 @@
     page_tables,
     context_lengths,
 ):
-    summed = lax.psum_scatter(
-        jnp.dot(merged_hidden, merger_weight, preferred_element_type=jnp.float32),
-        "seq",
-        scatter_dimension=0,
-        tiled=True,
-    )
-    image_rows = (summed + merger_bias).astype(jnp.bfloat16)
-    arrived = passed_along(image_rows, "section", 1)
-    embedded = place_images(text_embed, arrived, image_tokens[0], image_offsets[0])
-    widened = embedded.astype(jnp.float32)
-    squares = lax.psum(jnp.sum(widened * widened, axis=1), "tp")
-    scaling = lax.rsqrt(squares / D + EPSILON)[:, None]
-    normed_part = (widened * scaling * prefill_gain.astype(jnp.float32)).astype(jnp.bfloat16)
-    normed_all = lax.all_gather(normed_part, "tp", axis=1, tiled=True)
-    projected = (
-        jnp.dot(
-            normed_all,
-            lax.all_gather(kv_weight, "seq", axis=0, tiled=True),
-            preferred_element_type=jnp.float32,
-        )
-        + kv_bias
-    )
-    prompt_cache = rotate_keys(projected, HD)
-    fresh_rows = passed_along(prompt_cache, "section", 1)
-    section_count = lax.axis_size("section")
-    previous = (lax.axis_index("section") + section_count - 1) % section_count * lax.axis_size(
-        "seq"
-    ) + lax.axis_index("seq")
-    fresh_length = lax.dynamic_slice_in_dim(prompt_lengths, previous, 1, 0)
-    page_rows = cache_pages.shape[1]
-    pages_each = page_tables.shape[1]
-    fresh_pages = fresh_rows.reshape(pages_each, page_rows, fresh_rows.shape[1])
-    combined = jnp.concatenate([cache_pages, fresh_pages], axis=0)
-    appended = (cache_pages.shape[0] + jnp.arange(pages_each, dtype=jnp.int32))[None, :]
-    all_tables = jnp.concatenate([page_tables, appended], axis=0)
-    all_lengths = jnp.concatenate([context_lengths, fresh_length], axis=0)
-    decode_out = attend(queries, combined, all_tables, all_lengths, HD)
+    weight = lax.all_gather(kv_weight, "seq", axis=0, tiled=True)
+    image_rows = merged_images(merged_hidden, merger_weight, merger_bias)
+    text_all, gain_all = gathered_text(text_embed, prefill_gain)
+    resident = queries.shape[0] - 1
+    asked = hop(queries[resident:], -1, 0)
+    resident_out = attend(queries[:resident], cache_pages, page_tables, context_lengths, HD)
+    text_normed = normalized(text_all, gain_all)
+    image_normed = normalized(lax.all_gather(image_rows, "tp", axis=1, tiled=True), gain_all)
+    text_projected = jnp.dot(text_normed, weight, preferred_element_type=jnp.float32)
+    image_projected = jnp.dot(image_normed, weight, preferred_element_type=jnp.float32)
+    projected = placed(text_projected, image_projected, image_tokens[0], image_offsets[0])
+    prompt_cache = rotate_keys(projected + kv_bias, HD)
+    place = lax.axis_index("section") * lax.axis_size("seq") + lax.axis_index("seq")
+    length = lax.dynamic_slice_in_dim(prompt_lengths, place, 1, 0)[0]
+    fresh = attend_fresh(asked.reshape(-1, HD), prompt_cache, length, HD)
+    fresh_out = hop(fresh.reshape(1, -1), 1, 0)
+    decode_out = jnp.concatenate([resident_out, fresh_out], axis=0)
     return (prompt_cache, decode_out)
 
 

time: 243 us -> 160 us (0.66)
  waiting for transfers between devices: 172 us -> 10.6 us
  starting transfers between devices: 6.55 us -> 65.7 us
  other arithmetic: 6.76 us -> 18.8 us
  local copies, waits for them, and re-layouts: 9.9 us -> 14.4 us
  matrix products: 10.9 us -> 15.3 us
  blocking collectives: 22.9 us -> 18.5 us
    all_gather x2 -> x1, waiting for transfers between devices: 92 us -> 0.02 us  [per_device(): weight = lax.all_gather(kv_weight, 'seq', axis=0, tiled=True)]
    reduce_scatter x1 -> x0, waiting for transfers between devices: 71.5 us -> none  [per_device(): lax.psum_scatter(jnp.dot(merged_hidden, merger_weight, preferred_element_...]
    ppermute x2 -> x14, starting transfers between devices: 6.43 us -> 65.7 us  [the longest x10 51.1 us: hop(): return lax.ppermute(value, ('section', 'seq'), pairs)]
    psum x1 -> x0, blocking collectives: 22.9 us -> none  [per_device(): squares = lax.psum(jnp.sum(widened * widened, axis=1), 'tp')]
    all_gather x0 -> x1, blocking collectives: none -> 18.5 us  [per_device(): lax.all_gather(image_rows, 'tp', axis=1, tiled=True)]
    unnamed x0 -> x7, other arithmetic: none -> 6.15 us
    another operation x2 -> x4, other arithmetic: 0.5 us -> 6.55 us  [the longest x1 3.81 us: gathered_text(): both = jnp.stack([mine, others])]
    dot_general x2 -> x8, matrix products: 8.95 us -> 13.3 us  [the longest x1 5.55 us: per_device(): jnp.dot(text_normed, weight, preferred_element_type=jnp.float32)]
  transfers between devices with their start and end apart: 5 -> 15, of which waited for: 5 -> 3; matrix products, arithmetic and copies ran while one was open for 2% -> 20% of each run, Pallas kernels for 0% -> 0%
where the time goes in v1:
time: 160 us; the launch traced here: 158 us
  starting transfers between devices  65.7 us (41%)
  other arithmetic  18.8 us (12%)
  blocking collectives  18.5 us (12%)
  matrix products  15.3 us (10%)
  between operations  15.1 us (9%)
  local copies, waits for them, and re-layouts  14.4 us (9%)
  waiting for transfers between devices  10.6 us (7%)
    ppermute x10, starting transfers between devices, hop(): return lax.ppermute(value, ('section', 'seq'), pairs)  51.1 us
    all_gather x1, blocking collectives, per_device(): lax.all_gather(image_rows, 'tp', axis=1, tiled=True)  18.5 us
    ppermute x10, waiting for transfers between devices, hop(): return lax.ppermute(value, ('section', 'seq'), pairs)  10.6 us
    ppermute x3, starting transfers between devices, tp_hop(): lax.ppermute(value, 'tp', [(t, (t + steps) % count) for t in range(count)])  10.3 us
    gather x2, local copies, waits for them, and re-layouts, attend(): gathered = jnp.take(page_pool, page_table, axis=0)  6.97 us
    unnamed x7, other arithmetic  6.15 us
    dot_general x1, matrix products, per_device(): jnp.dot(text_normed, weight, preferred_element_type=jnp.float32)  5.55 us
    dot_general x4, matrix products, share(): jnp.dot(rows.reshape(192, rows.shape[2]), merger_weight, preferred_elemen...  4.27 us
  transfers between devices with their start and end apart: 15, of which 3 were waited for; matrix products, arithmetic and copies ran while one was open for 20% of the time, Pallas kernels for 0%

profile of v1, /device:TPU:1, one launch (start us, length us, event | category | flops | bytes accessed | tf_op | source)
XLA Modules:
  0.0 158.5 jit_solution(15859959469026018455)
XLA Ops:
  8.1 2.2 %fusion.48 = (bf16[1,272,1024]{2,1,0:T(8,128)(2,1)}, bf16[272,1024]{1,0:T(8,128)(2,1)}) fusion(bf16[16,1024]{1,0:T(8,128)(2,1)S(1)} %broadcast_in_dim.93, bf16[256,1024]{1,0:T(8,128)(2,1)} %param.17), kind=kLoop, calls=%fused_computation.124 | loop fusion | flops 1114112 | bytes 1671168 | tf_op jit(solution)/shard_map/stack | solution.py:79
  10.3 5.5 %collective-permute-start.8 = (bf16[272,1024]{1,0:T(8,128)(2,1)}, bf16[272,1024]{1,0:T(8,128)(2,1)}, u32[]{:S(2)}, u32[]{:S(2)}) collective-permute-start(bf16[272,1024]{1,0:T(8,128)(2,1)} %get-tuple-element.9), channel_id=1, source_target_pairs={{0,6},{1,7},{2,0},{3,1},{4,2},{5,3},{6,4},{7,5},{8,14},{9,15},{10,... | collective-permute-start | bytes 1671176 | tf_op jit(solution)/shard_map/ppermute | solution.py:30
  15.8 2.3 %collective-permute-start.9 = (bf16[272,1024]{1,0:T(8,128)(2,1)}, bf16[272,1024]{1,0:T(8,128)(2,1)}, u32[]{:S(2)}, u32[]{:S(2)}) collective-permute-start(bf16[272,1024]{1,0:T(8,128)(2,1)} %get-tuple-element.9), channel_id=1, source_target_pairs={{0,4},{1,5},{2,6},{3,7},{4,0},{5,1},{6,2},{7,3},{8,12},{9,13},{10,... | collective-permute-start | bytes 1671176 | tf_op jit(solution)/shard_map/ppermute | solution.py:30
  18.1 2.6 %collective-permute-start.10 = (bf16[272,1024]{1,0:T(8,128)(2,1)}, bf16[272,1024]{1,0:T(8,128)(2,1)}, u32[]{:S(2)}, u32[]{:S(2)}) collective-permute-start(bf16[272,1024]{1,0:T(8,128)(2,1)} %get-tuple-element.9), channel_id=1, source_target_pairs={{0,2},{1,3},{2,4},{3,5},{4,6},{5,7},{6,0},{7,1},{8,10},{9,11},{10,... | collective-permute-start | bytes 1671176 | tf_op jit(solution)/shard_map/ppermute | solution.py:30
  20.8 1.3 copy.22
  24.0 4.9 %collective-permute-start.2 = (bf16[192,512]{1,0:T(8,128)(2,1)}, bf16[192,512]{1,0:T(8,128)(2,1)}, u32[]{:S(2)}, u32[]{:S(2)}) collective-permute-start(bf16[192,512]{1,0:T(8,128)(2,1)} %get-tuple-element.14), channel_id=1, source_target_pairs={{0,16},{8,24},{16,32},{24,40},{32,48},{40,56},{48,64},{56,72},{64,... | collective-permute-start | bytes 589832 | tf_op jit(solution)/shard_map/ppermute | solution.py:25
  28.9 8.6 %collective-permute-start.3 = (bf16[192,512]{1,0:T(8,128)(2,1)}, bf16[192,512]{1,0:T(8,128)(2,1)}, u32[]{:S(2)}, u32[]{:S(2)}) collective-permute-start(bf16[192,512]{1,0:T(8,128)(2,1)} %get-tuple-element.15), channel_id=1, source_target_pairs={{0,112},{8,120},{16,0},{24,8},{32,16},{40,24},{48,32},{56,40},{64,... | collective-permute-start | bytes 589832 | tf_op jit(solution)/shard_map/ppermute | solution.py:25
  40.3 2.2 %gather_fusion.1 = bf16[240,16,256]{2,1,0:T(8,128)(2,1)} fusion(bf16[240,16,256]{2,1,0:T(8,128)(2,1)S(1)} %copy-done, s32[1024]{0:T(1024)S(1)} %pad_clamp_fusion), kind=kCustom, calls=%fused_computation.1 | custom fusion | bytes 3933120 | tf_op jit(solution)/shard_map/jit(_take)/gather | solution.py:144
  42.5 4.8 %gather.12 = bf16[15,256,1,2,128]{4,3,1,0,2:T(2,128)(2,1)} reshape(bf16[240,16,256]{2,1,0:T(8,128)(2,1)} %gather_fusion.1) | data formatting | bytes 3932160 | tf_op jit(solution)/shard_map/jit(_take)/gather | solution.py:144
  47.6 2.1 %copy_select_fusion = bf16[15,256,1,2,128]{4,1,0,3,2:T(8,128)(2,1)S(1)} fusion(bf16[15,256,1,2,128]{4,3,1,0,2:T(2,128)(2,1)} %gather.12, pred[15,256]{1,0:T(8,128)(4,1)S(1)} %broadcast_in_dim.97), kind=kLoop, calls=%fused_computation.29 | loop fusion | flops 983040 | bytes 3936000 | tf_op jit(solution)/shard_map/jit(_take)/select_n | solution.py:144
  49.7 2.6 %collective-permute-start = (bf16[192,1024]{1,0:T(8,128)(2,1)}, bf16[192,1024]{1,0:T(8,128)(2,1)}, u32[]{:S(2)}, u32[]{:S(2)}) collective-permute-start(bf16[192,1024]{1,0:T(8,128)(2,1)} %convolution_convert_fusion.2), channel_id=1, source_target_pairs={{0,8},{8,16},{16,24},{24,32},{32,40},{40,48},{48,56},{56,64},{64,7... | collective-permute-start | bytes 1179656 | tf_op jit(solution)/shard_map/ppermute | solution.py:25
  52.4 3.8 %collective-permute-start.1 = (bf16[192,1024]{1,0:T(8,128)(2,1)}, bf16[192,1024]{1,0:T(8,128)(2,1)}, u32[]{:S(2)}, u32[]{:S(2)}) collective-permute-start(bf16[192,1024]{1,0:T(8,128)(2,1)} %convolution_convert_fusion.1), channel_id=1, source_target_pairs={{0,120},{8,0},{16,8},{24,16},{32,24},{40,32},{48,40},{56,48},{64,5... | collective-permute-start | bytes 1179656 | tf_op jit(solution)/shard_map/ppermute | solution.py:25
  56.3 3.8 %fusion.49 = (bf16[1,4,272,1024]{3,2,1,0:T(8,128)(2,1)}, bf16[4,272,1024]{2,1,0:T(8,128)(2,1)}) fusion(bf16[1,272,1024]{2,1,0:T(8,128)(2,1)} %bitcast.16, bf16[1,272,1024]{2,1,0:T(8,128)(2,1)} %bitcast.15, bf16[1,272,1024]{2,1,0:T(8,128)(2,1)} %bitcast.14, bf16[1,272,1024]{2,1,0:T(8,128)(2,1)S(1)} %copy-done.4), kind=kLoop, calls=%fused_computation.125 | loop fusion | flops 3342336 | bytes 6684672 | tf_op jit(solution)/shard_map/stack | solution.py:81
  60.1 4.3 %collective-permute-start.11 = (bf16[4,272,1024]{2,1,0:T(8,128)(2,1)}, bf16[4,272,1024]{2,1,0:T(8,128)(2,1)}, u32[]{:S(2)}, u32[]{:S(2)}) collective-permute-start(bf16[4,272,1024]{2,1,0:T(8,128)(2,1)} %get-tuple-element.3), channel_id=1, source_target_pairs={{0,1},{1,0},{2,3},{3,2},{4,5},{5,4},{6,7},{7,6},{8,9},{9,8},{10,11... | collective-permute-start | bytes 6684680 | tf_op jit(solution)/shard_map/ppermute | solution.py:34
  66.5 4.4 %collective-permute-start.12 = (bf16[1,1024]{1,0:T(2,128)(2,1)S(1)}, bf16[1,1024]{1,0:T(2,128)(2,1)S(1)}, u32[]{:S(2)}, u32[]{:S(2)}) collective-permute-start(bf16[1,1024]{1,0:T(2,128)(2,1)S(1)} %slice.55), channel_id=1, source_target_pairs={{0,384},{8,392},{16,400},{24,408},{32,416},{40,424},{48,432},{56,4... | collective-permute-start | bytes 6152 | tf_op jit(solution)/shard_map/ppermute | solution.py:25
  70.9 1.6 %add_convert_fusion = bf16[192,1024]{1,0:T(8,128)(2,1)S(1)} fusion(bf16[192,1024]{1,0:T(8,128)(2,1)} %collective-permute-done.1, bf16[192,1024]{1,0:T(8,128)(2,1)} %collective-permute-done, bf16[192,512]{1,0:T(8,128)(2,1)} %collective-permute-done.3, bf16[192,512]{1,0:T(8,128)(2,1)} %collective-permute-done.2, bf16[192,320]{1,0:T(8,128)(2,1)S(1)} %bitcast.93, ...), kind=kOutput, calls=%fused_computation.55 | convolution fusion | flops 127795200 | bytes 2351104 | tf_op jit(solution)/shard_map/dot_general | solution.py:44
  72.6 12.1 %collective-permute-start.4 = (bf16[48,1024]{1,0:T(8,128)(2,1)S(1)}, bf16[48,1024]{1,0:T(8,128)(2,1)S(1)}, u32[]{:S(2)}, u32[]{:S(2)}) collective-permute-start(bf16[48,1024]{1,0:T(8,128)(2,1)S(1)} %get-tuple-element.10), channel_id=1, source_target_pairs={{0,192},{8,200},{16,208},{24,216},{32,224},{40,232},{48,240},{56,2... | collective-permute-start | bytes 294920 | tf_op jit(solution)/shard_map/ppermute | solution.py:25
  84.7 3.5 %collective-permute-start.5 = (bf16[48,1024]{1,0:T(8,128)(2,1)S(1)}, bf16[48,1024]{1,0:T(8,128)(2,1)S(1)}, u32[]{:S(2)}, u32[]{:S(2)}) collective-permute-start(bf16[48,1024]{1,0:T(8,128)(2,1)S(1)} %get-tuple-element.13), channel_id=1, source_target_pairs={{0,160},{8,168},{16,176},{24,184},{32,192},{40,200},{48,208},{56,2... | collective-permute-start | bytes 294920 | tf_op jit(solution)/shard_map/ppermute | solution.py:25
  88.2 7.4 %collective-permute-start.6 = (bf16[48,1024]{1,0:T(8,128)(2,1)S(1)}, bf16[48,1024]{1,0:T(8,128)(2,1)S(1)}, u32[]{:S(2)}, u32[]{:S(2)}) collective-permute-start(bf16[48,1024]{1,0:T(8,128)(2,1)S(1)} %get-tuple-element.12), channel_id=1, source_target_pairs={{0,224},{8,232},{16,240},{24,248},{32,128},{40,136},{48,144},{56,1... | collective-permute-start | bytes 294920 | tf_op jit(solution)/shard_map/ppermute | solution.py:25
  95.6 1.9 %collective-permute-start.7 = (bf16[48,1024]{1,0:T(8,128)(2,1)S(1)}, bf16[48,1024]{1,0:T(8,128)(2,1)S(1)}, u32[]{:S(2)}, u32[]{:S(2)}) collective-permute-start(bf16[48,1024]{1,0:T(8,128)(2,1)S(1)} %get-tuple-element.11), channel_id=1, source_target_pairs={{0,128},{8,136},{16,144},{24,152},{32,160},{40,168},{48,176},{56,1... | collective-permute-start | bytes 294920 | tf_op jit(solution)/shard_map/ppermute | solution.py:25
  98.2 5.2 %collective-permute-done.5 = bf16[48,1024]{1,0:T(8,128)(2,1)S(1)} collective-permute-done((bf16[48,1024]{1,0:T(8,128)(2,1)S(1)}, bf16[48,1024]{1,0:T(8,128)(2,1)S(1)}, u32[]{:S(2)}, u32[]{:S(2)}) %collective-permute-start.5) | collective-permute-done | bytes 98336 | tf_op jit(solution)/shard_map/ppermute | solution.py:25
  103.4 3.3 %collective-permute-done.6 = bf16[48,1024]{1,0:T(8,128)(2,1)S(1)} collective-permute-done((bf16[48,1024]{1,0:T(8,128)(2,1)S(1)}, bf16[48,1024]{1,0:T(8,128)(2,1)S(1)}, u32[]{:S(2)}, u32[]{:S(2)}) %collective-permute-start.6) | collective-permute-done | bytes 98336 | tf_op jit(solution)/shard_map/ppermute | solution.py:25
  106.8 18.5 %all_gather.6 = bf16[48,8192]{1,0:T(8,128)(2,1)S(1)} all-gather(bf16[48,1024]{1,0:T(8,128)(2,1)S(1)} %add_convert_fusion.1), channel_id=1, replica_groups=mesh['section'=4,'seq'=16,'tp'=8] {'tp'}, dimensions={1}, use_global_device_ids=true | all-gather | bytes 884736 | tf_op jit(solution)/shard_map/all_gather | solution.py:198
  125.6 1.5 bitcast_dynamic-update-slice_fusion.7
  127.7 1.3 bitcast_dynamic-update-slice_fusion.5
  129.2 1.3 bitcast_dynamic-update-slice_fusion.3
  130.8 1.3 bitcast_dynamic-update-slice_fusion.1
  134.4 3.1 %fusion.24 = f32[48,256]{1,0:T(8,128)S(1)} fusion(bf16[8192,256]{1,0:T(8,128)(2,1)} %all-gather.2.cloned.1.call-done, bf16[48,8192]{1,0:T(8,128)(2,1)S(1)} %all_gather.6, f32[8192]{0:T(1024)S(1)} %bitcast.100, f32[48]{0:T(128)S(1)} %add_rsqrt_fusion.1), kind=kOutput, calls=%fused_computation.52 | convolution fusion | flops 202899456 | bytes 5062848 | tf_op jit(solution)/shard_map/dot_general | solution.py:200
  138.7 5.6 %fusion.16 = f32[256,256]{0,1:T(8,128)S(1)} fusion(bf16[8192,256]{1,0:T(8,128)(2,1)} %all-gather.2.cloned.1.call-done, f32[8192]{0:T(1024)S(1)} %bitcast.101, f32[256]{0:T(256)S(1)} %add_rsqrt_fusion, bf16[272,8192]{1,0:T(8,128)(2,1)} %copy-done.3, f32[256,256]{0,1:T(8,128)S(1)} %copy.23, f32[256]{0:T(256)S(1)} %copy-done.14, ...), kind=kOutput, calls=%fused_computation.40 | convolution fusion | flops 1082327040 | bytes 8948224 | tf_op jit(solution)/shard_map/dot_general | solution.py:199
  145.4 1.9 %collective-permute-start.13 = (bf16[1,1024]{1,0:T(2,128)(2,1)S(1)}, bf16[1,1024]{1,0:T(2,128)(2,1)S(1)}, u32[]{:S(2)}, u32[]{:S(2)}) collective-permute-start(bf16[1,1024]{1,0:T(2,128)(2,1)S(1)} %bitcast.107), channel_id=1, source_target_pairs={{0,128},{8,136},{16,144},{24,152},{32,160},{40,168},{48,176},{56,1... | collective-permute-start | bytes 6152 | tf_op jit(solution)/shard_map/ppermute | solution.py:25
  147.3 1.6 convolution_convert_fusion.3
  148.9 2.0 %collective-permute-done.13 = bf16[1,1024]{1,0:T(2,128)(2,1)S(1)} collective-permute-done((bf16[1,1024]{1,0:T(2,128)(2,1)S(1)}, bf16[1,1024]{1,0:T(2,128)(2,1)S(1)}, u32[]{:S(2)}, u32[]{:S(2)}) %collective-permute-start.13) | collective-permute-done | bytes 2080 | tf_op jit(solution)/shard_map/ppermute | solution.py:25
  (102 shorter events, 14.9 us)
Async XLA Ops:
  7.2 33.1 %copy-start = (bf16[240,16,256]{2,1,0:T(8,128)(2,1)S(1)}, bf16[240,16,256]{2,1,0:T(8,128)(2,1)}, u32[]{:S(2)}) copy-start(bf16[240,16,256]{2,1,0:T(8,128)(2,1)} %param.25) | copy-start | bytes 5898244
  7.2 15.7 %copy-start.2 = (bf16[320,1024]{1,0:T(8,128)(2,1)S(1)}, bf16[320,1024]{1,0:T(8,128)(2,1)}, u32[]{:S(2)}) copy-start(bf16[320,1024]{1,0:T(8,128)(2,1)} %param.15) | copy-start | bytes 1966084
  7.2 127.3 %all-gather.2.cloned.1.call-start = ((), (), s32[]{:S(2)}) async-start(), calls=%async_computation | async-start | bytes 4456448 | tf_op jit(solution)/shard_map/all_gather | solution.py:191
  10.3 39.4 %collective-permute-start.8 = (bf16[272,1024]{1,0:T(8,128)(2,1)}, bf16[272,1024]{1,0:T(8,128)(2,1)}, u32[]{:S(2)}, u32[]{:S(2)}) collective-permute-start(bf16[272,1024]{1,0:T(8,128)(2,1)} %get-tuple-element.9), channel_id=1, source_target_pairs={{0,6},{1,7},{2,0},{3,1},{4,2},{5,3},{6,4},{7,5},{8,14},{9,15},{10,... | collective-permute-start | bytes 1671176 | tf_op jit(solution)/shard_map/ppermute | solution.py:30
  15.8 36.6 %collective-permute-start.9 = (bf16[272,1024]{1,0:T(8,128)(2,1)}, bf16[272,1024]{1,0:T(8,128)(2,1)}, u32[]{:S(2)}, u32[]{:S(2)}) collective-permute-start(bf16[272,1024]{1,0:T(8,128)(2,1)} %get-tuple-element.9), channel_id=1, source_target_pairs={{0,4},{1,5},{2,6},{3,7},{4,0},{5,1},{6,2},{7,3},{8,12},{9,13},{10,... | collective-permute-start | bytes 1671176 | tf_op jit(solution)/shard_map/ppermute | solution.py:30
  18.1 38.2 %collective-permute-start.10 = (bf16[272,1024]{1,0:T(8,128)(2,1)}, bf16[272,1024]{1,0:T(8,128)(2,1)}, u32[]{:S(2)}, u32[]{:S(2)}) collective-permute-start(bf16[272,1024]{1,0:T(8,128)(2,1)} %get-tuple-element.9), channel_id=1, source_target_pairs={{0,2},{1,3},{2,4},{3,5},{4,6},{5,7},{6,0},{7,1},{8,10},{9,11},{10,... | collective-permute-start | bytes 1671176 | tf_op jit(solution)/shard_map/ppermute | solution.py:30
  20.7 16.8 %copy-start.12 = (s32[1,4]{1,0:T(1,128)S(1)}, s32[1,4]{1,0:T(1,128)}, u32[]{:S(2)}) copy-start(s32[1,4]{1,0:T(1,128)} %param.18) | copy-start | bytes 52
  20.7 17.0 %copy-start.9 = (s32[15,16]{1,0:T(8,128)S(1)}, s32[15,16]{1,0:T(8,128)}, u32[]{:S(2)}) copy-start(s32[15,16]{1,0:T(8,128)} %param.26) | copy-start | bytes 2884
  20.7 17.0 %copy-start.11 = (s32[1,4]{1,0:T(1,128)S(1)}, s32[1,4]{1,0:T(1,128)}, u32[]{:S(2)}) copy-start(s32[1,4]{1,0:T(1,128)} %param.19) | copy-start | bytes 52
  22.9 15.2 %copy-start.6 = (bf16[4,1,48,320]{3,2,1,0:T(8,128)(2,1)S(1)}, bf16[4,1,48,320]{3,2,1,0:T(8,128)(2,1)}, u32[]{:S(2)}) copy-start(bf16[4,1,48,320]{3,2,1,0:T(8,128)(2,1)} %get-tuple-element.6) | copy-start | bytes 368644
  24.0 42.4 %collective-permute-start.2 = (bf16[192,512]{1,0:T(8,128)(2,1)}, bf16[192,512]{1,0:T(8,128)(2,1)}, u32[]{:S(2)}, u32[]{:S(2)}) collective-permute-start(bf16[192,512]{1,0:T(8,128)(2,1)} %get-tuple-element.14), channel_id=1, source_target_pairs={{0,16},{8,24},{16,32},{24,40},{32,48},{40,56},{48,64},{56,72},{64,... | collective-permute-start | bytes 589832 | tf_op jit(solution)/shard_map/ppermute | solution.py:25
  28.9 41.9 %collective-permute-start.3 = (bf16[192,512]{1,0:T(8,128)(2,1)}, bf16[192,512]{1,0:T(8,128)(2,1)}, u32[]{:S(2)}, u32[]{:S(2)}) collective-permute-start(bf16[192,512]{1,0:T(8,128)(2,1)} %get-tuple-element.15), channel_id=1, source_target_pairs={{0,112},{8,120},{16,0},{24,8},{32,16},{40,24},{48,32},{56,40},{64,... | collective-permute-start | bytes 589832 | tf_op jit(solution)/shard_map/ppermute | solution.py:25
  42.5 5.0 %copy-start.13 = (s32[15]{0:T(128)S(1)}, s32[15]{0:T(128)}, u32[]{:S(2)}) copy-start(s32[15]{0:T(128)} %param.27) | copy-start | bytes 184
  47.3 8.9 %copy-start.4 = (bf16[1,272,1024]{2,1,0:T(8,128)(2,1)S(1)}, bf16[1,272,1024]{2,1,0:T(8,128)(2,1)}, u32[]{:S(2)}) copy-start(bf16[1,272,1024]{2,1,0:T(8,128)(2,1)} %get-tuple-element.8) | copy-start | bytes 1671172
  49.7 14.7 %copy-start.5 = (bf16[15,256,1,2,128]{4,1,0,3,2:T(8,128)(2,1)}, bf16[15,256,1,2,128]{4,1,0,3,2:T(8,128)(2,1)S(1)}, u32[]{:S(2)}) copy-start(bf16[15,256,1,2,128]{4,1,0,3,2:T(8,128)(2,1)S(1)} %copy_select_fusion) | copy-start | bytes 5898244
  49.7 21.2 %collective-permute-start = (bf16[192,1024]{1,0:T(8,128)(2,1)}, bf16[192,1024]{1,0:T(8,128)(2,1)}, u32[]{:S(2)}, u32[]{:S(2)}) collective-permute-start(bf16[192,1024]{1,0:T(8,128)(2,1)} %convolution_convert_fusion.2), channel_id=1, source_target_pairs={{0,8},{8,16},{16,24},{24,32},{32,40},{40,48},{48,56},{56,64},{64,7... | collective-permute-start | bytes 1179656 | tf_op jit(solution)/shard_map/ppermute | solution.py:25
  52.4 18.5 %collective-permute-start.1 = (bf16[192,1024]{1,0:T(8,128)(2,1)}, bf16[192,1024]{1,0:T(8,128)(2,1)}, u32[]{:S(2)}, u32[]{:S(2)}) collective-permute-start(bf16[192,1024]{1,0:T(8,128)(2,1)} %convolution_convert_fusion.1), channel_id=1, source_target_pairs={{0,120},{8,0},{16,8},{24,16},{32,24},{40,32},{48,40},{56,48},{64,5... | collective-permute-start | bytes 1179656 | tf_op jit(solution)/shard_map/ppermute | solution.py:25
  56.2 8.1 %copy-start.8 = (bf16[16,1024]{1,0:T(8,128)(2,1)S(1)}, bf16[16,1024]{1,0:T(8,128)(2,1)}, u32[]{:S(2)}) copy-start(bf16[16,1024]{1,0:T(8,128)(2,1)} %param.24) | copy-start | bytes 98308
  56.3 8.9 %copy-start.15 = (s32[64]{0:T(128)S(1)}, s32[64]{0:T(128)}, u32[]{:S(2)}) copy-start(s32[64]{0:T(128)} %param.23) | copy-start | bytes 772
  60.1 65.5 %collective-permute-start.11 = (bf16[4,272,1024]{2,1,0:T(8,128)(2,1)}, bf16[4,272,1024]{2,1,0:T(8,128)(2,1)}, u32[]{:S(2)}, u32[]{:S(2)}) collective-permute-start(bf16[4,272,1024]{2,1,0:T(8,128)(2,1)} %get-tuple-element.3), channel_id=1, source_target_pairs={{0,1},{1,0},{2,3},{3,2},{4,5},{5,4},{6,7},{7,6},{8,9},{9,8},{10,11... | collective-permute-start | bytes 6684680 | tf_op jit(solution)/shard_map/ppermute | solution.py:34
  64.8 42.0 %copy-start.10 = (f32[1024]{0:T(1024)S(1)}, f32[1024]{0:T(1024)}, u32[]{:S(2)}) copy-start(f32[1024]{0:T(1024)} %param.16) | copy-start | bytes 12292
  66.5 29.1 %collective-permute-start.12 = (bf16[1,1024]{1,0:T(2,128)(2,1)S(1)}, bf16[1,1024]{1,0:T(2,128)(2,1)S(1)}, u32[]{:S(2)}, u32[]{:S(2)}) collective-permute-start(bf16[1,1024]{1,0:T(2,128)(2,1)S(1)} %slice.55), channel_id=1, source_target_pairs={{0,384},{8,392},{16,400},{24,408},{32,416},{40,424},{48,432},{56,4... | collective-permute-start | bytes 6152 | tf_op jit(solution)/shard_map/ppermute | solution.py:25
  72.6 25.6 %collective-permute-start.4 = (bf16[48,1024]{1,0:T(8,128)(2,1)S(1)}, bf16[48,1024]{1,0:T(8,128)(2,1)S(1)}, u32[]{:S(2)}, u32[]{:S(2)}) collective-permute-start(bf16[48,1024]{1,0:T(8,128)(2,1)S(1)} %get-tuple-element.10), channel_id=1, source_target_pairs={{0,192},{8,200},{16,208},{24,216},{32,224},{40,232},{48,240},{56,2... | collective-permute-start | bytes 294920 | tf_op jit(solution)/shard_map/ppermute | solution.py:25
  84.7 18.7 %collective-permute-start.5 = (bf16[48,1024]{1,0:T(8,128)(2,1)S(1)}, bf16[48,1024]{1,0:T(8,128)(2,1)S(1)}, u32[]{:S(2)}, u32[]{:S(2)}) collective-permute-start(bf16[48,1024]{1,0:T(8,128)(2,1)S(1)} %get-tuple-element.13), channel_id=1, source_target_pairs={{0,160},{8,168},{16,176},{24,184},{32,192},{40,200},{48,208},{56,2... | collective-permute-start | bytes 294920 | tf_op jit(solution)/shard_map/ppermute | solution.py:25
  88.2 18.5 %collective-permute-start.6 = (bf16[48,1024]{1,0:T(8,128)(2,1)S(1)}, bf16[48,1024]{1,0:T(8,128)(2,1)S(1)}, u32[]{:S(2)}, u32[]{:S(2)}) collective-permute-start(bf16[48,1024]{1,0:T(8,128)(2,1)S(1)} %get-tuple-element.12), channel_id=1, source_target_pairs={{0,224},{8,232},{16,240},{24,248},{32,128},{40,136},{48,144},{56,1... | collective-permute-start | bytes 294920 | tf_op jit(solution)/shard_map/ppermute | solution.py:25
  95.6 11.2 %collective-permute-start.7 = (bf16[48,1024]{1,0:T(8,128)(2,1)S(1)}, bf16[48,1024]{1,0:T(8,128)(2,1)S(1)}, u32[]{:S(2)}, u32[]{:S(2)}) collective-permute-start(bf16[48,1024]{1,0:T(8,128)(2,1)S(1)} %get-tuple-element.11), channel_id=1, source_target_pairs={{0,128},{8,136},{16,144},{24,152},{32,160},{40,168},{48,176},{56,1... | collective-permute-start | bytes 294920 | tf_op jit(solution)/shard_map/ppermute | solution.py:25
  125.6 1.8 %copy-start.1 = (bf16[1,4,272,1024]{3,2,1,0:T(8,128)(2,1)S(1)}, bf16[1,4,272,1024]{3,2,1,0:T(8,128)(2,1)}, u32[]{:S(2)}) copy-start(bf16[1,4,272,1024]{3,2,1,0:T(8,128)(2,1)} %get-tuple-element.2) | copy-start | bytes 6684676
  132.4 2.0 %copy-start.3 = (bf16[272,8192]{1,0:T(8,128)(2,1)}, bf16[272,8192]{1,0:T(8,128)(2,1)S(1)}, u32[]{:S(2)}) copy-start(bf16[272,8192]{1,0:T(8,128)(2,1)S(1)} %bitcast_dynamic-update-slice_fusion) | copy-start | bytes 13369348
  137.5 1.1 copy-start.14
  137.5 1.1 copy-start.16
  144.7 6.9 %copy-start.7 = (bf16[256,256]{1,0:T(8,128)(2,1)}, bf16[256,256]{1,0:T(8,128)(2,1)S(1)}, u32[]{:S(2)}) copy-start(bf16[256,256]{1,0:T(8,128)(2,1)S(1)} %copy.26) | copy-start | bytes 393220
  145.4 5.6 %collective-permute-start.13 = (bf16[1,1024]{1,0:T(2,128)(2,1)S(1)}, bf16[1,1024]{1,0:T(2,128)(2,1)S(1)}, u32[]{:S(2)}, u32[]{:S(2)}) collective-permute-start(bf16[1,1024]{1,0:T(2,128)(2,1)S(1)} %bitcast.107), channel_id=1, source_target_pairs={{0,128},{8,136},{16,144},{24,152},{32,160},{40,168},{48,176},{56,1... | collective-permute-start | bytes 6152 | tf_op jit(solution)/shard_map/ppermute | solution.py:25
Sparse Core Ops, SparseCore 0:
  37.7 91.8 all-gather.1

commit v2 on v0

v2 whole, which is shorter than its diff:
```python
import math

import jax
import jax.numpy as jnp
from jax import lax
from jax.experimental import pallas as pl
from jax.experimental.pallas import tpu as pltpu
from jax.sharding import PartitionSpec as P

D = 8192
TP = ("row", "core")
HD = 128
EPSILON = 1e-06
THETA = 1000000.0
MASKED = -1e30
F32 = jnp.float32
BF16 = jnp.bfloat16
SMALL = pl.CostEstimate(flops=1024, bytes_accessed=1024, transcendentals=0)
VMEM_BYTES = 32 * 1024 * 1024


def whole(memory_space=pltpu.VMEM):
    return pl.BlockSpec(memory_space=memory_space)


def hop(value, section_steps, seq_steps):
    sections = lax.axis_size("section")
    owners = lax.axis_size("seq")
    pairs = [
        (x * owners + z, (x + section_steps) % sections * owners + (z + seq_steps) % owners)
        for x in range(sections)
        for z in range(owners)
    ]
    return lax.ppermute(value, ("section", "seq"), pairs)


def after(value, *others):
    return lax.optimization_barrier((value,) + others)[0]


def wide(value):
    return value.astype(F32)


def shares_kernel(
    place_ref, hidden_ref, weight_ref, text_ref, gain_ref,
    far_ref, other_ref, near_ref, own_ref, sent_ref,
):
    weight = weight_ref[...]
    for step, out_ref in ((2, far_ref), (1, other_ref), (3, near_ref), (0, own_ref)):
        quarter = lax.rem(place_ref[0] + step, 4)
        for k in range(4):
            start = pl.multiple_of((4 * k + quarter) * 48, 16)
            out = jnp.dot(hidden_ref[pl.ds(start, 48), :], weight, preferred_element_type=F32)
            out_ref[pl.ds(48 * k, 48), :] = out.astype(out_ref.dtype)
    rows = text_ref.shape[0]
    gain = jnp.broadcast_to(wide(gain_ref[...]), (16, gain_ref.shape[1])).astype(BF16)
    for k in range(sent_ref.shape[0]):
        sent_ref[k, :rows, :] = text_ref[...]
        sent_ref[k, rows:, :] = gain


def merger_shares(merged_hidden, merger_weight, text_embed, gain):
    shape = (192, merger_weight.shape[1])
    rows, width = text_embed.shape
    shapes = [jax.ShapeDtypeStruct(shape, kind) for kind in (BF16, BF16, F32, F32)]
    shapes.append(jax.ShapeDtypeStruct((lax.axis_size("row"), rows + 16, width), BF16))
    return pl.pallas_call(
        shares_kernel,
        out_shape=tuple(shapes),
        in_specs=[whole(pltpu.SMEM)] + [whole()] * 4,
        out_specs=(whole(),) * 5,
        cost_estimate=SMALL,
        compiler_params=pltpu.CompilerParams(vmem_limit_bytes=VMEM_BYTES),
        name="merger_shares",
    )(lax.axis_index("seq")[None], merged_hidden, merger_weight, text_embed, gain[None, :])


def summed_images(shares, merger_bias, text, queries):
    z = lax.axis_index("seq")
    far, other, near, own = shares
    far = hop(far, 0, -1)
    other = hop(other, 0, 1)
    near = hop((near + wide(far)).astype(BF16), 0, -1)
    total = (own + wide(other) + wide(near)).reshape(4, 48, own.shape[1])
    total, text = lax.optimization_barrier((total, text))
    others = lax.ppermute(text, "core", [(0, 1), (1, 0)])

    def block(step):
        return lax.dynamic_index_in_dim(total, (z // 4 + step) % 4, axis=0, keepdims=False)

    far = hop(block(2).astype(BF16), 0, -4)
    other = hop(block(1).astype(BF16), 1, 4)
    own = hop((block(0) + merger_bias).astype(BF16), 1, 0)
    near = (wide(block(3)) + wide(far)).astype(BF16)
    near, text, others, queries = lax.optimization_barrier((near, text, others, queries))
    near = hop(near, 1, -4)
    return (wide(own) + wide(other) + wide(near)).astype(BF16), text, others, queries


def text_kernel(core_ref, mine_ref, others_ref, out_ref, gain_ref):
    rows = out_ref.shape[0]
    pieces, width = mine_ref.shape[0], mine_ref.shape[2]
    core = core_ref[0]
    sides = ((mine_ref, core), (others_ref, 1 - core))
    squares = jnp.zeros((rows, 1), F32)
    for ref, side in sides:
        for k in range(pieces):
            part = wide(ref[k, :rows, :])
            squares = squares + jnp.sum(part * part, axis=1, keepdims=True)
    scaling = lax.rsqrt(squares / D + EPSILON)
    for ref, side in sides:
        for k in range(pieces):
            columns = pl.ds(pl.multiple_of((2 * k + side) * width, width), width)
            gain = wide(ref[k, rows:, :])
            gain_ref[:, columns] = gain
            out_ref[:, columns] = (wide(ref[k, :rows, :]) * scaling * gain[:1]).astype(BF16)


def normed_text(mine, others):
    rows = mine.shape[1] - 16
    return pl.pallas_call(
        text_kernel,
        out_shape=(
            jax.ShapeDtypeStruct((rows, D), BF16),
            jax.ShapeDtypeStruct((16, D), F32),
        ),
        in_specs=[whole(pltpu.SMEM), whole(), whole()],
        out_specs=(whole(), whole()),
        cost_estimate=pl.CostEstimate(
            flops=20 * 1024 * 1024, bytes_accessed=9 * 1024 * 1024, transcendentals=0
        ),
        compiler_params=pltpu.CompilerParams(vmem_limit_bytes=VMEM_BYTES),
        name="text_norm",
    )(lax.axis_index("core")[None], mine, others)


def soft(scores, live):
    scores = jnp.where(live, scores / math.sqrt(HD), MASKED)
    weights = jnp.exp(scores - jnp.max(scores, axis=-1, keepdims=True))
    return (weights / jnp.sum(weights, axis=-1, keepdims=True)).astype(BF16)


def project_kernel(
    length_ref, counts_ref, starts_ref, image_ref, gain_ref, bias_ref, cos_ref,
    sin_ref, asked_ref, text_ref, weight_ref, cache_ref, fresh_ref,
    rows_ref, rows_arrived_ref, held_ref, arrived_ref,
):
    chunks, depth = held_ref.shape[0], held_ref.shape[1]
    copies = []
    for k in range(chunks):
        part = pl.ds(k * depth, depth)
        copies.append((
            pltpu.make_async_copy(text_ref.at[:, part], rows_ref.at[k], rows_arrived_ref.at[k]),
            pltpu.make_async_copy(weight_ref.at[part, :], held_ref.at[k], arrived_ref.at[k]),
        ))
    for of_text, of_weight in copies:
        of_text.start()
        of_weight.start()
    rows = cache_ref.shape[0]
    images = image_ref.shape[0]
    widened = wide(image_ref[...])
    scaling = lax.rsqrt(jnp.sum(widened * widened, axis=1, keepdims=True) / D + EPSILON)
    position = lax.broadcasted_iota(jnp.int32, (rows, images), 0)
    source = lax.broadcasted_iota(jnp.int32, (rows, images), 1)
    picks = jnp.zeros((rows, images), F32)
    earlier = jnp.int32(0)
    for k in range(4):
        start, count = starts_ref[k], counts_ref[k]
        inside = (position >= start) & (position < start + count)
        chosen = inside & (source == position - start + earlier)
        picks = picks + jnp.where(chosen, 1.0, 0.0)
        earlier = earlier + count
    covered = jnp.sum(picks, axis=1, keepdims=True) > 0.5
    picks = picks.astype(BF16)
    text_total = jnp.zeros((rows, cache_ref.shape[1]), F32)
    image_total = jnp.zeros((images, cache_ref.shape[1]), F32)
    for k, (of_text, of_weight) in enumerate(copies):
        of_text.wait()
        of_weight.wait()
        for first in range(0, depth, 256):
            columns = slice(k * depth + first, k * depth + first + 256)
            weight = held_ref[k, first : first + 256, :]
            normed = wide(image_ref[:, columns]) * scaling * gain_ref[:1, columns]
            text_total = text_total + jnp.dot(
                rows_ref[k, :, first : first + 256], weight, preferred_element_type=F32
            )
            image_total = image_total + jnp.dot(
                normed.astype(BF16), weight, preferred_element_type=F32
            )
    high = image_total.astype(BF16)
    rest = image_total - wide(high)
    middle = rest.astype(BF16)
    low = (rest - wide(middle)).astype(BF16)
    picked = jnp.dot(picks, high, preferred_element_type=F32)
    picked = picked + jnp.dot(picks, middle, preferred_element_type=F32)
    picked = picked + jnp.dot(picks, low, preferred_element_type=F32)
    projected = jnp.where(covered, picked, text_total) + bias_ref[...]
    keys = projected[:, :HD]
    turned = pltpu.roll(keys, HD // 2, axis=1)
    keys = (keys * cos_ref[...] + turned * sin_ref[...]).astype(BF16)
    values = projected[:, HD:].astype(BF16)
    cache_ref[:, :HD] = keys
    cache_ref[:, HD:] = values
    scores = lax.dot_general(
        asked_ref[...], keys, (((1,), (1,)), ((), ())), preferred_element_type=F32
    )
    live = lax.broadcasted_iota(jnp.int32, scores.shape, 1) < length_ref[0]
    mixed = jnp.dot(soft(scores, live), values, preferred_element_type=F32)
    fresh_ref[...] = mixed.astype(BF16)


def project(counts, starts, text, images, gain, weight, bias, asked, length):
    positions = text.shape[0]
    half = HD // 2
    frequency = THETA ** (-jnp.arange(half, dtype=F32) * 2.0 / HD)
    angles = jnp.arange(positions, dtype=F32)[:, None] * frequency[None, :]
    cosine, sine = jnp.cos(angles), jnp.sin(angles)
    cosine = jnp.concatenate([cosine, cosine], axis=1)
    sine = jnp.concatenate([-sine, sine], axis=1)
    chunks = 8
    columns = weight.shape[1]
    return pl.pallas_call(
        project_kernel,
        out_shape=(
            jax.ShapeDtypeStruct((positions, columns), BF16),
            jax.ShapeDtypeStruct(asked.shape, BF16),
        ),
        in_specs=[whole(pltpu.SMEM)] * 3 + [whole()] * 6 + [whole(pl.ANY)] * 2,
        out_specs=(whole(), whole()),
        scratch_shapes=[
            pltpu.VMEM((chunks, positions, D // chunks), BF16),
            pltpu.SemaphoreType.DMA((chunks,)),
            pltpu.VMEM((chunks, D // chunks, columns), BF16),
            pltpu.SemaphoreType.DMA((chunks,)),
        ],
        cost_estimate=SMALL,
        compiler_params=pltpu.CompilerParams(vmem_limit_bytes=60 * 1024 * 1024),
        name="project",
    )(length, counts, starts, images, gain, bias[None, :], cosine, sine, asked, text, weight)


def resident_kernel(tables_ref, lengths_ref, asked_ref, pages_ref, out_ref, scores_ref, mixed_ref):
    requests, pages = tables_ref.shape
    span = scores_ref.shape[1]
    positions = lax.broadcasted_iota(jnp.int32, (8, span), 1)

    def side(request, first):
        return jnp.concatenate(
            [
                pages_ref[tables_ref[request, k], :, first : first + HD]
                for k in range(pages)
            ],
            axis=0,
        )

    scores_ref[requests * 8 :, :] = jnp.zeros((8, span), F32)
    mixed_ref[requests * 8 :, :] = jnp.zeros((8, HD), F32)
    for request in range(requests):
        rows = pl.ds(request * 8, 8)
        scores = lax.dot_general(
            asked_ref[rows, :].astype(BF16),
            side(request, 0),
            (((1,), (1,)), ((), ())),
            preferred_element_type=F32,
        )
        scores_ref[rows, :] = jnp.where(
            positions < lengths_ref[request], scores / math.sqrt(HD), MASKED
        )
    scores = scores_ref[...]
    weights = jnp.exp(scores - jnp.max(scores, axis=-1, keepdims=True))
    scores_ref[...] = weights / jnp.sum(weights, axis=-1, keepdims=True)
    for request in range(requests):
        rows = pl.ds(request * 8, 8)
        mixed_ref[rows, :] = jnp.dot(
            scores_ref[rows, :].astype(BF16), side(request, HD), preferred_element_type=F32
        )
    out_ref[...] = mixed_ref[...].astype(BF16)


def attend_resident(queries, cache_pages, page_tables, context_lengths):
    heads = queries.size // HD
    span = page_tables.shape[1] * cache_pages.shape[1]
    out = pl.pallas_call(
        resident_kernel,
        out_shape=jax.ShapeDtypeStruct((heads, HD), BF16),
        in_specs=[whole(pltpu.SMEM), whole(pltpu.SMEM), whole(), whole()],
        out_specs=whole(),
        scratch_shapes=[pltpu.VMEM((heads, span), F32), pltpu.VMEM((heads, HD), F32)],
        cost_estimate=SMALL,
        compiler_params=pltpu.CompilerParams(vmem_limit_bytes=VMEM_BYTES),
        name="resident",
    )(page_tables, context_lengths, wide(queries).reshape(heads, HD), cache_pages)
    return out


def per_device(
    merged_hidden,
    merger_weight,
    merger_bias,
    text_embed,
    image_tokens,
    image_offsets,
    prefill_gain,
    kv_weight,
    kv_bias,
    prompt_lengths,
    queries,
    cache_pages,
    page_tables,
    context_lengths,
):
    weight = lax.all_gather(kv_weight, "seq", axis=0, tiled=True)
    *shares, text = merger_shares(merged_hidden, merger_weight, text_embed, prefill_gain)
    text = lax.all_to_all(text, "row", 0, 0, tiled=True)
    image_rows, text, others, queries = summed_images(shares, merger_bias, text, queries)
    text_normed, gain_all = normed_text(text, others)
    image_all = lax.all_gather(image_rows, TP, axis=1, tiled=True)
    resident = queries.shape[0] - 1
    asked = hop(queries[resident:].reshape(-1, HD), -1, 0)
    resident_out = attend_resident(queries, cache_pages, page_tables, context_lengths)
    place = lax.axis_index("section") * lax.axis_size("seq") + lax.axis_index("seq")
    length = lax.dynamic_slice_in_dim(prompt_lengths, place, 1, 0)
    prompt_cache, fresh = project(
        image_tokens[0], image_offsets[0], text_normed, image_all, gain_all, weight, kv_bias,
        asked, length,
    )
    fresh_out = hop(fresh, 1, 0).reshape(1, -1)
    last = jnp.arange(resident + 1, dtype=jnp.int32)[:, None] == resident
    decode_out = jnp.where(last, fresh_out, resident_out.reshape(queries.shape))
    return (prompt_cache, decode_out)


def solution(mesh):
    sections, owners, columns = mesh.devices.shape
    devices = mesh.devices.reshape(sections, owners, columns // 2, 2)
    mesh = jax.sharding.Mesh(devices, ("section", "seq") + TP)
    return jax.shard_map(
        per_device,
        mesh=mesh,
        in_specs=(
            P("section", "seq"),
            P("seq", TP),
            P(TP),
            P(("section", "seq"), TP),
            P(("section", "seq"), None),
            P(("section", "seq"), None),
            P(TP),
            P("seq", TP),
            P(TP),
            P(),
            P(("section", "seq"), TP),
            P(("section", "seq"), None, TP),
            P(("section", "seq"), None),
            P(("section", "seq")),
        ),
        out_specs=(P(("section", "seq"), TP), P(("section", "seq"), TP)),
        check_vma=False,
    )
```

time: 243 us -> 155 us (0.64)
  waiting for transfers between devices: 172 us -> 34.7 us
  starting transfers between devices: 6.55 us -> 58.1 us
  Pallas kernels: 0 us -> 14.8 us
  matrix products: 10.9 us -> 0 us
  blocking collectives: 22.9 us -> 17.2 us
  other arithmetic: 6.76 us -> 3.5 us
    all_gather x2 -> x1, waiting for transfers between devices: 92 us -> 0.01 us  [per_device(): weight = lax.all_gather(kv_weight, 'seq', axis=0, tiled=True)]
    reduce_scatter x1 -> x0, waiting for transfers between devices: 71.5 us -> none  [per_device(): lax.psum_scatter(jnp.dot(merged_hidden, merger_weight, preferred_element_...]
    ppermute x2 -> x10, starting transfers between devices: 6.43 us -> 53 us  [the longest x9 46.4 us: hop(): return lax.ppermute(value, ('section', 'seq'), pairs)]
    ppermute x2 -> x10, waiting for transfers between devices: 7.79 us -> 34 us  [the longest x9 34 us: hop(): return lax.ppermute(value, ('section', 'seq'), pairs)]
    psum x1 -> x0, blocking collectives: 22.9 us -> none  [per_device(): squares = lax.psum(jnp.sum(widened * widened, axis=1), 'tp')]
    all_gather x0 -> x1, blocking collectives: none -> 17.2 us  [per_device(): image_all = lax.all_gather(image_rows, TP, axis=1, tiled=True)]
    pallas_call x0 -> x4, Pallas kernels: none -> 14.8 us  [the longest x1 7.47 us: project(): pl.pallas_call(project_kernel, out_shape=(jax.ShapeDtypeStruct((positions...]
    dot_general x4 -> x0, matrix products: 10.9 us -> none  [the longest x1 5.24 us: per_device(): jnp.dot(normed_all, lax.all_gather(kv_weight, 'seq', axis=0, tiled=True),...]
  transfers between devices with their start and end apart: 5 -> 12, of which waited for: 5 -> 6; matrix products, arithmetic and copies ran while one was open for 2% -> 4% of each run, Pallas kernels for 0% -> 5%
where the time goes in v2:
time: 155 us; the launch traced here: 154 us
  starting transfers between devices  58.1 us (37%)
  waiting for transfers between devices  34.7 us (22%)
  blocking collectives  17.2 us (11%)
  Pallas kernels  14.8 us (10%)
  between operations  14.4 us (9%)
  local copies, waits for them, and re-layouts  11.3 us (7%)
  other arithmetic  3.5 us (2%)
    ppermute x9, starting transfers between devices, hop(): return lax.ppermute(value, ('section', 'seq'), pairs)  46.4 us
    ppermute x9, waiting for transfers between devices, hop(): return lax.ppermute(value, ('section', 'seq'), pairs)  34 us
    all_gather x1, blocking collectives, per_device(): image_all = lax.all_gather(image_rows, TP, axis=1, tiled=True)  17.2 us
    unnamed x29, local copies, waits for them, and re-layouts  9.9 us
    pallas_call x1, Pallas kernels, project(): pl.pallas_call(project_kernel, out_shape=(jax.ShapeDtypeStruct((positions...  7.47 us
    ppermute x1, starting transfers between devices, summed_images(): others = lax.ppermute(text, 'core', [(0, 1), (1, 0)])  6.6 us
    all_to_all x1, starting transfers between devices, per_device(): text = lax.all_to_all(text, 'row', 0, 0, tiled=True)  5.01 us
    pallas_call x1, Pallas kernels, normed_text(): pl.pallas_call(text_kernel, out_shape=(jax.ShapeDtypeStruct((rows, D), BF...  3.95 us
  transfers between devices with their start and end apart: 12, of which 6 were waited for; matrix products, arithmetic and copies ran while one was open for 4% of the time, Pallas kernels for 5%

profile of v2, /device:TPU:1, one launch (start us, length us, event | category | flops | bytes accessed | tf_op | source)
XLA Modules:
  0.0 154.0 jit_solution(2325220793681976845)
XLA Ops:
  7.9 1.3 copy.16.hidden_ref
  9.2 0.7 broadcast_in_dim.35.gain_ref
  9.9 1.1 copy-done.4
  11.0 1.0 copy-done.6
  12.1 2.0 %merger_shares.1 = (bf16[192,1024]{1,0:T(8,128)(2,1)S(1)}, bf16[192,1024]{1,0:T(8,128)(2,1)S(1)}, f32[192,1024]{1,0:T(8,128)S(1)}, f32[192,1024]{1,0:T(8,128)S(1)}, bf16[4,272,1024]{2,1,0:T(8,128)(2,1)S(1)}) custom-call(s32[1]{0:T(128)} %bitcast.2.place_ref, bf16[768,320]{1,0:T(8,128)(2,1)S(1)} %copy.16.hidden_ref, bf16[320,1024]{1,0:T(8,128)(2,1)S(1)} %copy-done.4, ...), custom_call_target="tpu_custom_call" | custom-call | flops 1024 | bytes 1024 | tf_op jit(solution)/shard_map/merger_shares/pallas_call | solution.py:68
  14.1 1.4 copy-done.1
  15.5 0.9 copy-done.3
  16.4 0.7 copy-done.9
  17.1 5.0 %all-to-all-start = ((bf16[4,272,1024]{2,1,0:T(8,128)(2,1)}), bf16[4,272,1024]{2,1,0:T(8,128)(2,1)S(1)}, u32[]{:S(2)}, u32[]{:S(2)}) async-start(bf16[4,272,1024]{2,1,0:T(8,128)(2,1)} %copy-done.1), calls=%async_computation | async-start | bytes 4456448 | tf_op jit(solution)/shard_map/all_to_all | solution.py:315
  22.1 11.2 %collective-permute-start.1 = (bf16[192,1024]{1,0:T(8,128)(2,1)}, bf16[192,1024]{1,0:T(8,128)(2,1)S(1)}, u32[]{:S(2)}, u32[]{:S(2)}) collective-permute-start(bf16[192,1024]{1,0:T(8,128)(2,1)} %copy-done.9), channel_id=1, source_target_pairs={{0,120},{8,0},{16,8},{24,16},{32,24},{40,32},{48,40},{56,48},{64,5... | collective-permute-start | bytes 1179656 | tf_op jit(solution)/shard_map/ppermute | solution.py:34
  33.4 1.9 %collective-permute-start = (bf16[192,1024]{1,0:T(8,128)(2,1)S(1)}, bf16[192,1024]{1,0:T(8,128)(2,1)S(1)}, u32[]{:S(2)}, u32[]{:S(2)}) collective-permute-start(bf16[192,1024]{1,0:T(8,128)(2,1)S(1)} %get-tuple-element.18), channel_id=1, source_target_pairs={{0,8},{8,16},{16,24},{24,32},{32,40},{40,48},{48,56},{56,64},{64,7... | collective-permute-start | bytes 1179656 | tf_op jit(solution)/shard_map/ppermute | solution.py:34
  35.3 11.6 %collective-permute-done.1 = bf16[192,1024]{1,0:T(8,128)(2,1)S(1)} collective-permute-done((bf16[192,1024]{1,0:T(8,128)(2,1)}, bf16[192,1024]{1,0:T(8,128)(2,1)S(1)}, u32[]{:S(2)}, u32[]{:S(2)}) %collective-permute-start.1) | collective-permute-done | bytes 393248 | tf_op jit(solution)/shard_map/ppermute | solution.py:34
  47.0 5.3 %collective-permute-start.2 = (bf16[192,1024]{1,0:T(8,128)(2,1)S(1)}, bf16[192,1024]{1,0:T(8,128)(2,1)S(1)}, u32[]{:S(2)}, u32[]{:S(2)}) collective-permute-start(bf16[192,1024]{1,0:T(8,128)(2,1)S(1)} %add_convert_fusion), channel_id=1, source_target_pairs={{0,120},{8,0},{16,8},{24,16},{32,24},{40,32},{48,40},{56,48},{64,5... | collective-permute-start | bytes 1179656 | tf_op jit(solution)/shard_map/ppermute | solution.py:34
  52.3 1.9 %collective-permute-done = bf16[192,1024]{1,0:T(8,128)(2,1)S(1)} collective-permute-done((bf16[192,1024]{1,0:T(8,128)(2,1)S(1)}, bf16[192,1024]{1,0:T(8,128)(2,1)S(1)}, u32[]{:S(2)}, u32[]{:S(2)}) %collective-permute-start) | collective-permute-done | bytes 393248 | tf_op jit(solution)/shard_map/ppermute | solution.py:34
  54.3 12.2 %collective-permute-done.2 = bf16[192,1024]{1,0:T(8,128)(2,1)S(1)} collective-permute-done((bf16[192,1024]{1,0:T(8,128)(2,1)S(1)}, bf16[192,1024]{1,0:T(8,128)(2,1)S(1)}, u32[]{:S(2)}, u32[]{:S(2)}) %collective-permute-start.2) | collective-permute-done | bytes 393248 | tf_op jit(solution)/shard_map/ppermute | solution.py:34
  66.5 1.3 convert_add_fusion
  67.8 6.6 %collective-permute-start.6 = (bf16[4,272,1024]{2,1,0:T(8,128)(2,1)S(1)}, bf16[4,272,1024]{2,1,0:T(8,128)(2,1)}, u32[]{:S(2)}, u32[]{:S(2)}) collective-permute-start(bf16[4,272,1024]{2,1,0:T(8,128)(2,1)S(1)} %all-to-all-done.mine_ref), channel_id=1, source_target_pairs={{0,1},{1,0},{2,3},{3,2},{4,5},{5,4},{6,7},{7,6},{8,9},{9,8},{10,11... | collective-permute-start | bytes 6684680 | tf_op jit(solution)/shard_map/ppermute | solution.py:87
  75.7 7.4 %collective-permute-start.5 = (bf16[48,1024]{1,0:T(8,128)(2,1)S(1)}, bf16[48,1024]{1,0:T(8,128)(2,1)S(1)}, u32[]{:S(2)}, u32[]{:S(2)}) collective-permute-start(bf16[48,1024]{1,0:T(8,128)(2,1)S(1)} %get-tuple-element.35), channel_id=1, source_target_pairs={{0,96},{8,104},{16,112},{24,120},{32,0},{40,8},{48,16},{56,24},{64... | collective-permute-start | bytes 294920 | tf_op jit(solution)/shard_map/ppermute | solution.py:34
  83.1 0.8 pad_maximum_fusion
  84.0 2.7 %collective-permute-start.4 = (bf16[48,1024]{1,0:T(8,128)(2,1)S(1)}, bf16[48,1024]{1,0:T(8,128)(2,1)S(1)}, u32[]{:S(2)}, u32[]{:S(2)}) collective-permute-start(bf16[48,1024]{1,0:T(8,128)(2,1)S(1)} %get-tuple-element.34), channel_id=1, source_target_pairs={{0,160},{8,168},{16,176},{24,184},{32,192},{40,200},{48,208},{56,2... | collective-permute-start | bytes 294920 | tf_op jit(solution)/shard_map/ppermute | solution.py:34
  86.6 5.7 %collective-permute-done.5 = bf16[48,1024]{1,0:T(8,128)(2,1)S(1)} collective-permute-done((bf16[48,1024]{1,0:T(8,128)(2,1)S(1)}, bf16[48,1024]{1,0:T(8,128)(2,1)S(1)}, u32[]{:S(2)}, u32[]{:S(2)}) %collective-permute-start.5) | collective-permute-done | bytes 98336 | tf_op jit(solution)/shard_map/ppermute | solution.py:34
  92.4 3.1 %collective-permute-start.3 = (bf16[48,1024]{1,0:T(8,128)(2,1)S(1)}, bf16[48,1024]{1,0:T(8,128)(2,1)S(1)}, u32[]{:S(2)}, u32[]{:S(2)}) collective-permute-start(bf16[48,1024]{1,0:T(8,128)(2,1)S(1)} %get-tuple-element.32), channel_id=1, source_target_pairs={{0,128},{8,136},{16,144},{24,152},{32,160},{40,168},{48,176},{56,1... | collective-permute-start | bytes 294920 | tf_op jit(solution)/shard_map/ppermute | solution.py:34
  95.5 9.4 %collective-permute-start.7 = (bf16[48,1024]{1,0:T(8,128)(2,1)S(1)}, bf16[48,1024]{1,0:T(8,128)(2,1)S(1)}, u32[]{:S(2)}, u32[]{:S(2)}) collective-permute-start(bf16[48,1024]{1,0:T(8,128)(2,1)S(1)} %get-tuple-element.24), channel_id=1, source_target_pairs={{0,224},{8,232},{16,240},{24,248},{32,128},{40,136},{48,144},{56,1... | collective-permute-start | bytes 294920 | tf_op jit(solution)/shard_map/ppermute | solution.py:34
  105.0 3.3 %collective-permute-start.8 = (bf16[8,128]{1,0:T(8,128)(2,1)S(1)}, bf16[8,128]{1,0:T(8,128)(2,1)S(1)}, u32[]{:S(2)}, u32[]{:S(2)}) collective-permute-start(bf16[8,128]{1,0:T(8,128)(2,1)S(1)} %bitcast.22), channel_id=1, source_target_pairs={{0,384},{8,392},{16,400},{24,408},{32,416},{40,424},{48,432},{56,4... | collective-permute-start | bytes 6152 | tf_op jit(solution)/shard_map/ppermute | solution.py:34
  108.3 4.0 %text_norm.1 = (bf16[256,8192]{1,0:T(8,128)(2,1)S(1)}, f32[16,8192]{1,0:T(8,128)S(1)}) custom-call(s32[1]{0:T(128)} %bitcast.8.core_ref, bf16[4,272,1024]{2,1,0:T(8,128)(2,1)S(1)} %all-to-all-done.mine_ref, bf16[4,272,1024]{2,1,0:T(8,128)(2,1)} %collective-permute-done.6.others_ref), custom_call_target="tpu_custom_call" | custom-call | flops 20971520 | bytes 9437184 | tf_op jit(solution)/shard_map/text_norm/pallas_call | solution.py:122
  112.3 2.0 %copy-done = bf16[256,8192]{1,0:T(8,128)(2,1)} copy-done((bf16[256,8192]{1,0:T(8,128)(2,1)}, bf16[256,8192]{1,0:T(8,128)(2,1)S(1)}, u32[]{:S(2)}) %copy-start) | copy-done | bytes 4194328
  114.3 0.8 copy-done.5
  115.4 17.2 %all_gather.6.image_ref = bf16[48,8192]{1,0:T(8,128)(2,1)} all-gather(bf16[48,1024]{1,0:T(8,128)(2,1)S(1)} %add_convert_fusion.1), channel_id=1, replica_groups=mesh['section'=4,'seq'=16,'row'=4,'core'=2] {'row','core'}, dimensions={1}, use_global_device_ids=true | all-gather | bytes 884736 | tf_op jit(solution)/shard_map/all_gather | solution.py:318
  133.2 7.5 %project.1 = (bf16[256,256]{1,0:T(8,128)(2,1)}, bf16[8,128]{1,0:T(8,128)(2,1)}) custom-call(s32[1]{0:T(128)} %dynamic_slice.16.length_ref, s32[4]{0:T(128)} %bitcast.25, s32[4]{0:T(128)} %bitcast.26, bf16[48,8192]{1,0:T(8,128)(2,1)} %all_gather.6.image_ref, f32[16,8192]{1,0:T(8,128)} %copy-done.5, f32[1,256]{1,0:T(1,128)} %bitcast.24, ...), custom_call_target="tpu_custom_call" | custom-call | flops 1024 | bytes 1024 | tf_op jit(solution)/shard_map/project/pallas_call | solution.py:223
  140.7 1.9 %collective-permute-start.9 = (bf16[8,128]{1,0:T(8,128)(2,1)}, bf16[8,128]{1,0:T(8,128)(2,1)S(1)}, u32[]{:S(2)}, u32[]{:S(2)}) collective-permute-start(bf16[8,128]{1,0:T(8,128)(2,1)} %get-tuple-element.31), channel_id=1, source_target_pairs={{0,128},{8,136},{16,144},{24,152},{32,160},{40,168},{48,176},{56,1... | collective-permute-start | bytes 6152 | tf_op jit(solution)/shard_map/ppermute | solution.py:34
  142.7 1.3 resident.1
  144.1 2.3 %collective-permute-done.9 = bf16[8,128]{1,0:T(8,128)(2,1)S(1)} collective-permute-done((bf16[8,128]{1,0:T(8,128)(2,1)}, bf16[8,128]{1,0:T(8,128)(2,1)S(1)}, u32[]{:S(2)}, u32[]{:S(2)}) %collective-permute-start.9) | collective-permute-done | bytes 2080 | tf_op jit(solution)/shard_map/ppermute | solution.py:34
  (42 shorter events, 3.7 us)
Async XLA Ops:
  7.2 125.5 %all-gather.2.cloned.1.call-start = ((), (), s32[]{:S(2)}) async-start(), calls=%async_computation.1 | async-start | bytes 4456448 | tf_op jit(solution)/shard_map/all_gather | solution.py:313
  9.9 1.1 copy-start.4
  11.0 1.0 copy-start.6
  14.1 1.4 copy-start.1
  15.5 0.9 copy-start.3
  16.4 0.7 copy-start.9
  17.1 50.7 %all-to-all-start = ((bf16[4,272,1024]{2,1,0:T(8,128)(2,1)}), bf16[4,272,1024]{2,1,0:T(8,128)(2,1)S(1)}, u32[]{:S(2)}, u32[]{:S(2)}) async-start(bf16[4,272,1024]{2,1,0:T(8,128)(2,1)} %copy-done.1), calls=%async_computation | async-start | bytes 4456448 | tf_op jit(solution)/shard_map/all_to_all | solution.py:315
  22.1 52.4 %copy-start.13 = (s32[64]{0:T(128)S(1)}, s32[64]{0:T(128)}, u32[]{:S(2)}) copy-start(s32[64]{0:T(128)} %param.23) | copy-start | bytes 772
  22.1 24.8 %collective-permute-start.1 = (bf16[192,1024]{1,0:T(8,128)(2,1)}, bf16[192,1024]{1,0:T(8,128)(2,1)S(1)}, u32[]{:S(2)}, u32[]{:S(2)}) collective-permute-start(bf16[192,1024]{1,0:T(8,128)(2,1)} %copy-done.9), channel_id=1, source_target_pairs={{0,120},{8,0},{16,8},{24,16},{32,24},{40,32},{48,40},{56,48},{64,5... | collective-permute-start | bytes 1179656 | tf_op jit(solution)/shard_map/ppermute | solution.py:34
  33.4 20.9 %collective-permute-start = (bf16[192,1024]{1,0:T(8,128)(2,1)S(1)}, bf16[192,1024]{1,0:T(8,128)(2,1)S(1)}, u32[]{:S(2)}, u32[]{:S(2)}) collective-permute-start(bf16[192,1024]{1,0:T(8,128)(2,1)S(1)} %get-tuple-element.18), channel_id=1, source_target_pairs={{0,8},{8,16},{16,24},{24,32},{32,40},{40,48},{48,56},{56,64},{64,7... | collective-permute-start | bytes 1179656 | tf_op jit(solution)/shard_map/ppermute | solution.py:34
  47.0 45.3 %copy-start.11 = (f32[1024]{0:T(1024)S(1)}, f32[1024]{0:T(1024)}, u32[]{:S(2)}) copy-start(f32[1024]{0:T(1024)} %param.16) | copy-start | bytes 12292
  47.0 19.5 %collective-permute-start.2 = (bf16[192,1024]{1,0:T(8,128)(2,1)S(1)}, bf16[192,1024]{1,0:T(8,128)(2,1)S(1)}, u32[]{:S(2)}, u32[]{:S(2)}) collective-permute-start(bf16[192,1024]{1,0:T(8,128)(2,1)S(1)} %add_convert_fusion), channel_id=1, source_target_pairs={{0,120},{8,0},{16,8},{24,16},{32,24},{40,32},{48,40},{56,48},{64,5... | collective-permute-start | bytes 1179656 | tf_op jit(solution)/shard_map/ppermute | solution.py:34
  66.5 38.5 %copy-start.10 = (bf16[16,1024]{1,0:T(8,128)(2,1)S(1)}, bf16[16,1024]{1,0:T(8,128)(2,1)}, u32[]{:S(2)}) copy-start(bf16[16,1024]{1,0:T(8,128)(2,1)} %param.24) | copy-start | bytes 98308
  67.8 27.7 %collective-permute-start.6 = (bf16[4,272,1024]{2,1,0:T(8,128)(2,1)S(1)}, bf16[4,272,1024]{2,1,0:T(8,128)(2,1)}, u32[]{:S(2)}, u32[]{:S(2)}) collective-permute-start(bf16[4,272,1024]{2,1,0:T(8,128)(2,1)S(1)} %all-to-all-done.mine_ref), channel_id=1, source_target_pairs={{0,1},{1,0},{2,3},{3,2},{4,5},{5,4},{6,7},{7,6},{8,9},{9,8},{10,11... | collective-permute-start | bytes 6684680 | tf_op jit(solution)/shard_map/ppermute | solution.py:87
  75.7 16.6 %collective-permute-start.5 = (bf16[48,1024]{1,0:T(8,128)(2,1)S(1)}, bf16[48,1024]{1,0:T(8,128)(2,1)S(1)}, u32[]{:S(2)}, u32[]{:S(2)}) collective-permute-start(bf16[48,1024]{1,0:T(8,128)(2,1)S(1)} %get-tuple-element.35), channel_id=1, source_target_pairs={{0,96},{8,104},{16,112},{24,120},{32,0},{40,8},{48,16},{56,24},{64... | collective-permute-start | bytes 294920 | tf_op jit(solution)/shard_map/ppermute | solution.py:34
  84.0 31.2 %collective-permute-start.4 = (bf16[48,1024]{1,0:T(8,128)(2,1)S(1)}, bf16[48,1024]{1,0:T(8,128)(2,1)S(1)}, u32[]{:S(2)}, u32[]{:S(2)}) collective-permute-start(bf16[48,1024]{1,0:T(8,128)(2,1)S(1)} %get-tuple-element.34), channel_id=1, source_target_pairs={{0,160},{8,168},{16,176},{24,184},{32,192},{40,200},{48,208},{56,2... | collective-permute-start | bytes 294920 | tf_op jit(solution)/shard_map/ppermute | solution.py:34
  92.4 22.8 %collective-permute-start.3 = (bf16[48,1024]{1,0:T(8,128)(2,1)S(1)}, bf16[48,1024]{1,0:T(8,128)(2,1)S(1)}, u32[]{:S(2)}, u32[]{:S(2)}) collective-permute-start(bf16[48,1024]{1,0:T(8,128)(2,1)S(1)} %get-tuple-element.32), channel_id=1, source_target_pairs={{0,128},{8,136},{16,144},{24,152},{32,160},{40,168},{48,176},{56,1... | collective-permute-start | bytes 294920 | tf_op jit(solution)/shard_map/ppermute | solution.py:34
  95.5 19.8 %collective-permute-start.7 = (bf16[48,1024]{1,0:T(8,128)(2,1)S(1)}, bf16[48,1024]{1,0:T(8,128)(2,1)S(1)}, u32[]{:S(2)}, u32[]{:S(2)}) collective-permute-start(bf16[48,1024]{1,0:T(8,128)(2,1)S(1)} %get-tuple-element.24), channel_id=1, source_target_pairs={{0,224},{8,232},{16,240},{24,248},{32,128},{40,136},{48,144},{56,1... | collective-permute-start | bytes 294920 | tf_op jit(solution)/shard_map/ppermute | solution.py:34
  105.0 27.6 %collective-permute-start.8 = (bf16[8,128]{1,0:T(8,128)(2,1)S(1)}, bf16[8,128]{1,0:T(8,128)(2,1)S(1)}, u32[]{:S(2)}, u32[]{:S(2)}) collective-permute-start(bf16[8,128]{1,0:T(8,128)(2,1)S(1)} %bitcast.22), channel_id=1, source_target_pairs={{0,384},{8,392},{16,400},{24,408},{32,416},{40,424},{48,432},{56,4... | collective-permute-start | bytes 6152 | tf_op jit(solution)/shard_map/ppermute | solution.py:34
  112.3 2.0 %copy-start = (bf16[256,8192]{1,0:T(8,128)(2,1)}, bf16[256,8192]{1,0:T(8,128)(2,1)S(1)}, u32[]{:S(2)}) copy-start(bf16[256,8192]{1,0:T(8,128)(2,1)S(1)} %get-tuple-element.29.text_ref) | copy-start | bytes 12582916
  114.3 0.8 copy-start.5
  132.6 0.6 copy-start.12
  133.2 9.5 %copy-start.2 = (bf16[240,16,256]{2,1,0:T(8,128)(2,1)S(1)}, bf16[240,16,256]{2,1,0:T(8,128)(2,1)}, u32[]{:S(2)}) copy-start(bf16[240,16,256]{2,1,0:T(8,128)(2,1)} %pages_ref.1) | copy-start | bytes 5898244
  133.2 9.5 %copy-start.7 = (s32[15,16]{1,0:T(8,128)S(1)}, s32[15,16]{1,0:T(8,128)}, u32[]{:S(2)}) copy-start(s32[15,16]{1,0:T(8,128)} %tables_ref.1) | copy-start | bytes 2884
  133.2 9.5 %copy-start.8 = (s32[15]{0:T(128)S(1)}, s32[15]{0:T(128)}, u32[]{:S(2)}) copy-start(s32[15]{0:T(128)} %lengths_ref.1) | copy-start | bytes 184
  140.7 5.8 %collective-permute-start.9 = (bf16[8,128]{1,0:T(8,128)(2,1)}, bf16[8,128]{1,0:T(8,128)(2,1)S(1)}, u32[]{:S(2)}, u32[]{:S(2)}) collective-permute-start(bf16[8,128]{1,0:T(8,128)(2,1)} %get-tuple-element.31), channel_id=1, source_target_pairs={{0,128},{8,136},{16,144},{24,152},{32,160},{40,168},{48,176},{56,1... | collective-permute-start | bytes 6152 | tf_op jit(solution)/shard_map/ppermute | solution.py:34
Sparse Core Ops, SparseCore 0:
  10.1 97.2 all-gather.1

commit v3 on v2

--- a/solution.py
+++ b/solution.py
@@ -84,7 +84,7 @@
     near = hop((near + wide(far)).astype(BF16), 0, -1)
     total = (own + wide(other) + wide(near)).reshape(4, 48, own.shape[1])
     total, text = lax.optimization_barrier((total, text))
-    others = lax.ppermute(text, "core", [(0, 1), (1, 0)])
+    text = lax.all_to_all(text, "row", 0, 0, tiled=True)
 
     def block(step):
         return lax.dynamic_index_in_dim(total, (z // 4 + step) % 4, axis=0, keepdims=False)
@@ -93,46 +93,12 @@
     other = hop(block(1).astype(BF16), 1, 4)
     own = hop((block(0) + merger_bias).astype(BF16), 1, 0)
     near = (wide(block(3)) + wide(far)).astype(BF16)
-    near, text, others, queries = lax.optimization_barrier((near, text, others, queries))
+    queries = after(queries, near)
     near = hop(near, 1, -4)
-    return (wide(own) + wide(other) + wide(near)).astype(BF16), text, others, queries
-
-
-def text_kernel(core_ref, mine_ref, others_ref, out_ref, gain_ref):
-    rows = out_ref.shape[0]
-    pieces, width = mine_ref.shape[0], mine_ref.shape[2]
-    core = core_ref[0]
-    sides = ((mine_ref, core), (others_ref, 1 - core))
-    squares = jnp.zeros((rows, 1), F32)
-    for ref, side in sides:
-        for k in range(pieces):
-            part = wide(ref[k, :rows, :])
-            squares = squares + jnp.sum(part * part, axis=1, keepdims=True)
-    scaling = lax.rsqrt(squares / D + EPSILON)
-    for ref, side in sides:
-        for k in range(pieces):
-            columns = pl.ds(pl.multiple_of((2 * k + side) * width, width), width)
-            gain = wide(ref[k, rows:, :])
-            gain_ref[:, columns] = gain
-            out_ref[:, columns] = (wide(ref[k, :rows, :]) * scaling * gain[:1]).astype(BF16)
-
-
-def normed_text(mine, others):
-    rows = mine.shape[1] - 16
-    return pl.pallas_call(
-        text_kernel,
-        out_shape=(
-            jax.ShapeDtypeStruct((rows, D), BF16),
-            jax.ShapeDtypeStruct((16, D), F32),
-        ),
-        in_specs=[whole(pltpu.SMEM), whole(), whole()],
-        out_specs=(whole(), whole()),
-        cost_estimate=pl.CostEstimate(
-            flops=20 * 1024 * 1024, bytes_accessed=9 * 1024 * 1024, transcendentals=0
-        ),
-        compiler_params=pltpu.CompilerParams(vmem_limit_bytes=VMEM_BYTES),
-        name="text_norm",
-    )(lax.axis_index("core")[None], mine, others)
+    rows = (wide(own) + wide(other) + wide(near)).astype(BF16)
+    rows, text = lax.optimization_barrier((rows, text))
+    others = lax.ppermute(text, "core", [(0, 1), (1, 0)])
+    return rows, text, others, queries
 
 
 def soft(scores, live):
@@ -142,21 +108,18 @@
 
 
 def project_kernel(
-    length_ref, counts_ref, starts_ref, image_ref, gain_ref, bias_ref, cos_ref,
-    sin_ref, asked_ref, text_ref, weight_ref, cache_ref, fresh_ref,
-    rows_ref, rows_arrived_ref, held_ref, arrived_ref,
+    length_ref, core_ref, counts_ref, starts_ref, mine_ref, others_ref, image_ref, bias_ref,
+    cos_ref, sin_ref, asked_ref, weight_ref, cache_ref, fresh_ref, held_ref, arrived_ref,
 ):
     chunks, depth = held_ref.shape[0], held_ref.shape[1]
-    copies = []
-    for k in range(chunks):
-        part = pl.ds(k * depth, depth)
-        copies.append((
-            pltpu.make_async_copy(text_ref.at[:, part], rows_ref.at[k], rows_arrived_ref.at[k]),
-            pltpu.make_async_copy(weight_ref.at[part, :], held_ref.at[k], arrived_ref.at[k]),
-        ))
-    for of_text, of_weight in copies:
-        of_text.start()
-        of_weight.start()
+    copies = [
+        pltpu.make_async_copy(
+            weight_ref.at[pl.ds(k * depth, depth), :], held_ref.at[k], arrived_ref.at[k]
+        )
+        for k in range(chunks)
+    ]
+    for copy in copies:
+        copy.start()
     rows = cache_ref.shape[0]
     images = image_ref.shape[0]
     widened = wide(image_ref[...])
@@ -173,21 +136,34 @@
         earlier = earlier + count
     covered = jnp.sum(picks, axis=1, keepdims=True) > 0.5
     picks = picks.astype(BF16)
+    core = core_ref[0]
+    sides = ((mine_ref, core), (others_ref, 1 - core))
+    squares = jnp.zeros((rows, 1), F32)
+    for ref, side in sides:
+        for row in range(chunks // 2):
+            part = wide(ref[row, :rows, :])
+            squares = squares + jnp.sum(part * part, axis=1, keepdims=True)
+    text_scaling = lax.rsqrt(squares / D + EPSILON)
     text_total = jnp.zeros((rows, cache_ref.shape[1]), F32)
     image_total = jnp.zeros((images, cache_ref.shape[1]), F32)
-    for k, (of_text, of_weight) in enumerate(copies):
-        of_text.wait()
-        of_weight.wait()
-        for first in range(0, depth, 256):
-            columns = slice(k * depth + first, k * depth + first + 256)
-            weight = held_ref[k, first : first + 256, :]
-            normed = wide(image_ref[:, columns]) * scaling * gain_ref[:1, columns]
-            text_total = text_total + jnp.dot(
-                rows_ref[k, :, first : first + 256], weight, preferred_element_type=F32
-            )
-            image_total = image_total + jnp.dot(
-                normed.astype(BF16), weight, preferred_element_type=F32
-            )
+    for row in range(chunks // 2):
+        copies[2 * row].wait()
+        copies[2 * row + 1].wait()
+        for ref, side in sides:
+            chunk = 2 * row + side
+            for first in range(0, depth, 256):
+                part = slice(first, first + 256)
+                columns = pl.ds(pl.multiple_of(chunk * depth + first, 256), 256)
+                gain = wide(ref[row, rows:, part])[:1]
+                weight = held_ref[chunk, part, :]
+                normed = wide(ref[row, :rows, part]) * text_scaling * gain
+                text_total = text_total + jnp.dot(
+                    normed.astype(BF16), weight, preferred_element_type=F32
+                )
+                normed = wide(image_ref[:, columns]) * scaling * gain
+                image_total = image_total + jnp.dot(
+                    normed.astype(BF16), weight, preferred_element_type=F32
+                )
     high = image_total.astype(BF16)
     rest = image_total - wide(high)
     middle = rest.astype(BF16)
@@ -210,8 +186,8 @@
     fresh_ref[...] = mixed.astype(BF16)
 
 
-def project(counts, starts, text, images, gain, weight, bias, asked, length):
-    positions = text.shape[0]
+def project(counts, starts, mine, others, images, weight, bias, asked, length):
+    positions = mine.shape[1] - 16
     half = HD // 2
     frequency = THETA ** (-jnp.arange(half, dtype=F32) * 2.0 / HD)
     angles = jnp.arange(positions, dtype=F32)[:, None] * frequency[None, :]
@@ -226,18 +202,19 @@
             jax.ShapeDtypeStruct((positions, columns), BF16),
             jax.ShapeDtypeStruct(asked.shape, BF16),
         ),
-        in_specs=[whole(pltpu.SMEM)] * 3 + [whole()] * 6 + [whole(pl.ANY)] * 2,
+        in_specs=[whole(pltpu.SMEM)] * 4 + [whole()] * 7 + [whole(pl.ANY)],
         out_specs=(whole(), whole()),
         scratch_shapes=[
-            pltpu.VMEM((chunks, positions, D // chunks), BF16),
-            pltpu.SemaphoreType.DMA((chunks,)),
             pltpu.VMEM((chunks, D // chunks, columns), BF16),
             pltpu.SemaphoreType.DMA((chunks,)),
         ],
         cost_estimate=SMALL,
-        compiler_params=pltpu.CompilerParams(vmem_limit_bytes=60 * 1024 * 1024),
+        compiler_params=pltpu.CompilerParams(vmem_limit_bytes=VMEM_BYTES),
         name="project",
-    )(length, counts, starts, images, gain, bias[None, :], cosine, sine, asked, text, weight)
+    )(
+        length, lax.axis_index("core")[None], counts, starts, mine, others, images,
+        bias[None, :], cosine, sine, asked, weight,
+    )
 
 
 def resident_kernel(tables_ref, lengths_ref, asked_ref, pages_ref, out_ref, scores_ref, mixed_ref):
@@ -312,9 +289,7 @@
 ):
     weight = lax.all_gather(kv_weight, "seq", axis=0, tiled=True)
     *shares, text = merger_shares(merged_hidden, merger_weight, text_embed, prefill_gain)
-    text = lax.all_to_all(text, "row", 0, 0, tiled=True)
     image_rows, text, others, queries = summed_images(shares, merger_bias, text, queries)
-    text_normed, gain_all = normed_text(text, others)
     image_all = lax.all_gather(image_rows, TP, axis=1, tiled=True)
     resident = queries.shape[0] - 1
     asked = hop(queries[resident:].reshape(-1, HD), -1, 0)
@@ -322,8 +297,7 @@
     place = lax.axis_index("section") * lax.axis_size("seq") + lax.axis_index("seq")
     length = lax.dynamic_slice_in_dim(prompt_lengths, place, 1, 0)
     prompt_cache, fresh = project(
-        image_tokens[0], image_offsets[0], text_normed, image_all, gain_all, weight, kv_bias,
-        asked, length,
+        image_tokens[0], image_offsets[0], text, others, image_all, weight, kv_bias, asked, length
     )
     fresh_out = hop(fresh, 1, 0).reshape(1, -1)
     last = jnp.arange(resident + 1, dtype=jnp.int32)[:, None] == resident

time: 155 us -> 145 us (0.935)
  waiting for transfers between devices: 34.7 us -> 40.4 us
  starting transfers between devices: 58.1 us -> 53.9 us
  Pallas kernels: 14.8 us -> 10.7 us
  blocking collectives: 17.2 us -> 14.3 us
  local copies, waits for them, and re-layouts: 11.3 us -> 8.61 us
  other arithmetic: 3.5 us -> 1.65 us
    ppermute x9, starting transfers between devices: 46.4 us -> 40.1 us  [hop(): return lax.ppermute(value, ('section', 'seq'), pairs)]
    ppermute x9, waiting for transfers between devices: 34 us -> 39.7 us  [hop(): return lax.ppermute(value, ('section', 'seq'), pairs)]
    pallas_call x1 -> x0, Pallas kernels: 3.95 us -> none  [normed_text(): pl.pallas_call(text_kernel, out_shape=(jax.ShapeDtypeStruct((rows, D), BF...]
    all_gather x1, blocking collectives: 17.2 us -> 14.3 us  [per_device(): image_all = lax.all_gather(image_rows, TP, axis=1, tiled=True)]
    unnamed x29 -> x27, local copies, waits for them, and re-layouts: 9.9 us -> 7.22 us
  transfers between devices with their start and end apart: 12 -> 12, of which waited for: 6 -> 6; matrix products, arithmetic and copies ran while one was open for 4% -> 3% of each run, Pallas kernels for 5% -> 2%
where the time goes in v3:
time: 145 us; the launch traced here: 144 us
  starting transfers between devices  53.9 us (37%)
  waiting for transfers between devices  40.4 us (28%)
  between operations  14.5 us (10%)
  blocking collectives  14.3 us (10%)
  Pallas kernels  10.7 us (7%)
  local copies, waits for them, and re-layouts  8.61 us (6%)
  other arithmetic  1.65 us (1%)
    ppermute x9, starting transfers between devices, hop(): return lax.ppermute(value, ('section', 'seq'), pairs)  40.1 us
    ppermute x9, waiting for transfers between devices, hop(): return lax.ppermute(value, ('section', 'seq'), pairs)  39.7 us
    all_gather x1, blocking collectives, per_device(): image_all = lax.all_gather(image_rows, TP, axis=1, tiled=True)  14.3 us
    ppermute x1, starting transfers between devices, summed_images(): others = lax.ppermute(text, 'core', [(0, 1), (1, 0)])  7.84 us
    pallas_call x1, Pallas kernels, project(): pl.pallas_call(project_kernel, out_shape=(jax.ShapeDtypeStruct((positions...  7.37 us
    unnamed x27, local copies, waits for them, and re-layouts  7.22 us
    all_to_all x1, starting transfers between devices, summed_images(): text = lax.all_to_all(text, 'row', 0, 0, tiled=True)  5.95 us
  transfers between devices with their start and end apart: 12, of which 6 were waited for; matrix products, arithmetic and copies ran while one was open for 3% of the time, Pallas kernels for 2%

profile of v3, /device:TPU:1, one launch (start us, length us, event | category | flops | bytes accessed | tf_op | source)
XLA Modules:
  0.0 144.1 jit_solution(3107958267258773157)
XLA Ops:
  7.2 0.7 all-gather.2.cloned.1.call-update
  7.9 1.3 copy.16.hidden_ref
  9.2 0.7 broadcast_in_dim.36.gain_ref
  9.9 1.1 copy-done.3
  11.0 1.0 copy-done.4
  12.1 2.0 %merger_shares.1 = (bf16[192,1024]{1,0:T(8,128)(2,1)S(1)}, bf16[192,1024]{1,0:T(8,128)(2,1)S(1)}, f32[192,1024]{1,0:T(8,128)S(1)}, f32[192,1024]{1,0:T(8,128)S(1)}, bf16[4,272,1024]{2,1,0:T(8,128)(2,1)S(1)}) custom-call(s32[1]{0:T(128)} %bitcast.3.place_ref, bf16[768,320]{1,0:T(8,128)(2,1)S(1)} %copy.16.hidden_ref, bf16[320,1024]{1,0:T(8,128)(2,1)S(1)} %copy-done.3, ...), custom_call_target="tpu_custom_call" | custom-call | flops 1024 | bytes 1024 | tf_op jit(solution)/shard_map/merger_shares/pallas_call | solution.py:68
  14.1 11.9 %collective-permute-start.1 = (bf16[192,1024]{1,0:T(8,128)(2,1)S(1)}, bf16[192,1024]{1,0:T(8,128)(2,1)S(1)}, u32[]{:S(2)}, u32[]{:S(2)}) collective-permute-start(bf16[192,1024]{1,0:T(8,128)(2,1)S(1)} %get-tuple-element.17), channel_id=1, source_target_pairs={{0,120},{8,0},{16,8},{24,16},{32,24},{40,32},{48,40},{56,48},{64,5... | collective-permute-start | bytes 1179656 | tf_op jit(solution)/shard_map/ppermute | solution.py:34
  26.0 1.9 %collective-permute-start = (bf16[192,1024]{1,0:T(8,128)(2,1)S(1)}, bf16[192,1024]{1,0:T(8,128)(2,1)S(1)}, u32[]{:S(2)}, u32[]{:S(2)}) collective-permute-start(bf16[192,1024]{1,0:T(8,128)(2,1)S(1)} %get-tuple-element.15), channel_id=1, source_target_pairs={{0,8},{8,16},{16,24},{24,32},{32,40},{40,48},{48,56},{56,64},{64,7... | collective-permute-start | bytes 1179656 | tf_op jit(solution)/shard_map/ppermute | solution.py:34
  28.0 7.3 %collective-permute-done.1 = bf16[192,1024]{1,0:T(8,128)(2,1)S(1)} collective-permute-done((bf16[192,1024]{1,0:T(8,128)(2,1)S(1)}, bf16[192,1024]{1,0:T(8,128)(2,1)S(1)}, u32[]{:S(2)}, u32[]{:S(2)}) %collective-permute-start.1) | collective-permute-done | bytes 393248 | tf_op jit(solution)/shard_map/ppermute | solution.py:34
  35.4 5.4 %collective-permute-start.2 = (bf16[192,1024]{1,0:T(8,128)(2,1)S(1)}, bf16[192,1024]{1,0:T(8,128)(2,1)S(1)}, u32[]{:S(2)}, u32[]{:S(2)}) collective-permute-start(bf16[192,1024]{1,0:T(8,128)(2,1)S(1)} %add_convert_fusion), channel_id=1, source_target_pairs={{0,120},{8,0},{16,8},{24,16},{32,24},{40,32},{48,40},{56,48},{64,5... | collective-permute-start | bytes 1179656 | tf_op jit(solution)/shard_map/ppermute | solution.py:34
  40.8 0.4 collective-permute-done
  41.2 14.4 %collective-permute-done.2 = bf16[192,1024]{1,0:T(8,128)(2,1)S(1)} collective-permute-done((bf16[192,1024]{1,0:T(8,128)(2,1)S(1)}, bf16[192,1024]{1,0:T(8,128)(2,1)S(1)}, u32[]{:S(2)}, u32[]{:S(2)}) %collective-permute-start.2) | collective-permute-done | bytes 393248 | tf_op jit(solution)/shard_map/ppermute | solution.py:34
  55.5 0.1 convert_add_fusion
  55.7 6.0 %all-to-all-start = ((bf16[4,272,1024]{2,1,0:T(8,128)(2,1)}), bf16[4,272,1024]{2,1,0:T(8,128)(2,1)S(1)}, u32[]{:S(2)}, u32[]{:S(2)}) async-start(bf16[4,272,1024]{2,1,0:T(8,128)(2,1)} %copy-done.1), calls=%async_computation | async-start | bytes 4456448 | tf_op jit(solution)/shard_map/all_to_all | solution.py:87
  61.8 2.0 %collective-permute-start.5 = (bf16[48,1024]{1,0:T(8,128)(2,1)S(1)}, bf16[48,1024]{1,0:T(8,128)(2,1)S(1)}, u32[]{:S(2)}, u32[]{:S(2)}) collective-permute-start(bf16[48,1024]{1,0:T(8,128)(2,1)S(1)} %get-tuple-element.29), channel_id=1, source_target_pairs={{0,96},{8,104},{16,112},{24,120},{32,0},{40,8},{48,16},{56,24},{64... | collective-permute-start | bytes 294920 | tf_op jit(solution)/shard_map/ppermute | solution.py:34
  63.8 8.2 %collective-permute-start.4 = (bf16[48,1024]{1,0:T(8,128)(2,1)S(1)}, bf16[48,1024]{1,0:T(8,128)(2,1)S(1)}, u32[]{:S(2)}, u32[]{:S(2)}) collective-permute-start(bf16[48,1024]{1,0:T(8,128)(2,1)S(1)} %get-tuple-element.28), channel_id=1, source_target_pairs={{0,160},{8,168},{16,176},{24,184},{32,192},{40,200},{48,208},{56,2... | collective-permute-start | bytes 294920 | tf_op jit(solution)/shard_map/ppermute | solution.py:34
  72.0 3.9 %collective-permute-done.5 = bf16[48,1024]{1,0:T(8,128)(2,1)S(1)} collective-permute-done((bf16[48,1024]{1,0:T(8,128)(2,1)S(1)}, bf16[48,1024]{1,0:T(8,128)(2,1)S(1)}, u32[]{:S(2)}, u32[]{:S(2)}) %collective-permute-start.5) | collective-permute-done | bytes 98336 | tf_op jit(solution)/shard_map/ppermute | solution.py:34
  76.0 3.3 %collective-permute-start.3 = (bf16[48,1024]{1,0:T(8,128)(2,1)S(1)}, bf16[48,1024]{1,0:T(8,128)(2,1)S(1)}, u32[]{:S(2)}, u32[]{:S(2)}) collective-permute-start(bf16[48,1024]{1,0:T(8,128)(2,1)S(1)} %get-tuple-element.26), channel_id=1, source_target_pairs={{0,128},{8,136},{16,144},{24,152},{32,160},{40,168},{48,176},{56,1... | collective-permute-start | bytes 294920 | tf_op jit(solution)/shard_map/ppermute | solution.py:34
  79.4 1.9 %collective-permute-start.6 = (bf16[48,1024]{1,0:T(8,128)(2,1)S(1)}, bf16[48,1024]{1,0:T(8,128)(2,1)S(1)}, u32[]{:S(2)}, u32[]{:S(2)}) collective-permute-start(bf16[48,1024]{1,0:T(8,128)(2,1)S(1)} %get-tuple-element.27), channel_id=1, source_target_pairs={{0,224},{8,232},{16,240},{24,248},{32,128},{40,136},{48,144},{56,1... | collective-permute-start | bytes 294920 | tf_op jit(solution)/shard_map/ppermute | solution.py:34
  81.3 1.9 %collective-permute-done.3 = bf16[48,1024]{1,0:T(8,128)(2,1)S(1)} collective-permute-done((bf16[48,1024]{1,0:T(8,128)(2,1)S(1)}, bf16[48,1024]{1,0:T(8,128)(2,1)S(1)}, u32[]{:S(2)}, u32[]{:S(2)}) %collective-permute-start.3) | collective-permute-done | bytes 98336 | tf_op jit(solution)/shard_map/ppermute | solution.py:34
  83.2 11.8 %collective-permute-done.6 = bf16[48,1024]{1,0:T(8,128)(2,1)S(1)} collective-permute-done((bf16[48,1024]{1,0:T(8,128)(2,1)S(1)}, bf16[48,1024]{1,0:T(8,128)(2,1)S(1)}, u32[]{:S(2)}, u32[]{:S(2)}) %collective-permute-start.6) | collective-permute-done | bytes 98336 | tf_op jit(solution)/shard_map/ppermute | solution.py:34
  95.1 7.8 %collective-permute-start.7 = (bf16[4,272,1024]{2,1,0:T(8,128)(2,1)S(1)}, bf16[4,272,1024]{2,1,0:T(8,128)(2,1)}, u32[]{:S(2)}, u32[]{:S(2)}) collective-permute-start(bf16[4,272,1024]{2,1,0:T(8,128)(2,1)S(1)} %all-to-all-done.mine_ref), channel_id=1, source_target_pairs={{0,1},{1,0},{2,3},{3,2},{4,5},{5,4},{6,7},{7,6},{8,9},{9,8},{10,11... | collective-permute-start | bytes 6684680 | tf_op jit(solution)/shard_map/ppermute | solution.py:100
  102.9 0.6 dynamic_slice.16.length_ref
  103.5 0.5 fusion.6
  104.2 2.0 %collective-permute-start.8 = (bf16[8,128]{1,0:T(8,128)(2,1)S(1)}, bf16[8,128]{1,0:T(8,128)(2,1)S(1)}, u32[]{:S(2)}, u32[]{:S(2)}) collective-permute-start(bf16[8,128]{1,0:T(8,128)(2,1)S(1)} %bitcast.26), channel_id=1, source_target_pairs={{0,384},{8,392},{16,400},{24,408},{32,416},{40,424},{48,432},{56,4... | collective-permute-start | bytes 6152 | tf_op jit(solution)/shard_map/ppermute | solution.py:34
  106.2 14.3 %all_gather.6.image_ref = bf16[48,8192]{1,0:T(8,128)(2,1)S(1)} all-gather(bf16[48,1024]{1,0:T(8,128)(2,1)S(1)} %add_convert_fusion.1), channel_id=1, replica_groups=mesh['section'=4,'seq'=16,'row'=4,'core'=2] {'row','core'}, dimensions={1}, use_global_device_ids=true | all-gather | bytes 884736 | tf_op jit(solution)/shard_map/all_gather | solution.py:293
  120.6 2.2 %copy-done = bf16[8192,256]{1,0:T(8,128)(2,1)S(1)} copy-done((bf16[8192,256]{1,0:T(8,128)(2,1)S(1)}, bf16[8192,256]{1,0:T(8,128)(2,1)}, u32[]{:S(2)}) %copy-start) | copy-done | bytes 4194328
  122.8 7.4 %project.1 = (bf16[256,256]{1,0:T(8,128)(2,1)}, bf16[8,128]{1,0:T(8,128)(2,1)S(1)}) custom-call(s32[1]{0:T(128)} %dynamic_slice.16.length_ref, s32[1]{0:T(128)} %bitcast.core_ref, s32[4]{0:T(128)S(1)} %bitcast.21, s32[4]{0:T(128)S(1)} %bitcast.22, bf16[4,272,1024]{2,1,0:T(8,128)(2,1)S(1)} %all-to-all-done.mine_ref, ...), custom_call_target="tpu_custom_call" | custom-call | flops 1024 | bytes 1024 | tf_op jit(solution)/shard_map/project/pallas_call | solution.py:199
  130.2 3.3 %collective-permute-start.9 = (bf16[8,128]{1,0:T(8,128)(2,1)S(1)}, bf16[8,128]{1,0:T(8,128)(2,1)S(1)}, u32[]{:S(2)}, u32[]{:S(2)}) collective-permute-start(bf16[8,128]{1,0:T(8,128)(2,1)S(1)} %get-tuple-element.25), channel_id=1, source_target_pairs={{0,128},{8,136},{16,144},{24,152},{32,160},{40,168},{48,176},{56,1... | collective-permute-start | bytes 6152 | tf_op jit(solution)/shard_map/ppermute | solution.py:34
  133.6 1.5 %copy-done.2 = bf16[240,16,256]{2,1,0:T(8,128)(2,1)S(1)} copy-done((bf16[240,16,256]{2,1,0:T(8,128)(2,1)S(1)}, bf16[240,16,256]{2,1,0:T(8,128)(2,1)}, u32[]{:S(2)}) %copy-start.2) | copy-done | bytes 1966104
  135.1 1.3 resident.1
  136.5 0.7 broadcast_select_fusion
  (39 shorter events, 0.5 us)
Async XLA Ops:
  7.2 113.4 %all-gather.2.cloned.1.call-start = ((), (), s32[]{:S(2)}) async-start(), calls=%async_computation.1 | async-start | bytes 4456448 | tf_op jit(solution)/shard_map/all_gather | solution.py:290
  9.9 1.1 copy-start.3
  11.0 1.0 copy-start.4
  14.1 41.6 %copy-start.1 = (bf16[4,272,1024]{2,1,0:T(8,128)(2,1)}, bf16[4,272,1024]{2,1,0:T(8,128)(2,1)S(1)}, u32[]{:S(2)}) copy-start(bf16[4,272,1024]{2,1,0:T(8,128)(2,1)S(1)} %get-tuple-element.20) | copy-start | bytes 6684676
  14.1 21.2 %collective-permute-start.1 = (bf16[192,1024]{1,0:T(8,128)(2,1)S(1)}, bf16[192,1024]{1,0:T(8,128)(2,1)S(1)}, u32[]{:S(2)}, u32[]{:S(2)}) collective-permute-start(bf16[192,1024]{1,0:T(8,128)(2,1)S(1)} %get-tuple-element.17), channel_id=1, source_target_pairs={{0,120},{8,0},{16,8},{24,16},{32,24},{40,32},{48,40},{56,48},{64,5... | collective-permute-start | bytes 1179656 | tf_op jit(solution)/shard_map/ppermute | solution.py:34
  26.0 15.1 %collective-permute-start = (bf16[192,1024]{1,0:T(8,128)(2,1)S(1)}, bf16[192,1024]{1,0:T(8,128)(2,1)S(1)}, u32[]{:S(2)}, u32[]{:S(2)}) collective-permute-start(bf16[192,1024]{1,0:T(8,128)(2,1)S(1)} %get-tuple-element.15), channel_id=1, source_target_pairs={{0,8},{8,16},{16,24},{24,32},{32,40},{40,48},{48,56},{56,64},{64,7... | collective-permute-start | bytes 1179656 | tf_op jit(solution)/shard_map/ppermute | solution.py:34
  35.4 20.1 %collective-permute-start.2 = (bf16[192,1024]{1,0:T(8,128)(2,1)S(1)}, bf16[192,1024]{1,0:T(8,128)(2,1)S(1)}, u32[]{:S(2)}, u32[]{:S(2)}) collective-permute-start(bf16[192,1024]{1,0:T(8,128)(2,1)S(1)} %add_convert_fusion), channel_id=1, source_target_pairs={{0,120},{8,0},{16,8},{24,16},{32,24},{40,32},{48,40},{56,48},{64,5... | collective-permute-start | bytes 1179656 | tf_op jit(solution)/shard_map/ppermute | solution.py:34
  55.7 20.3 %copy-start.11 = (f32[1024]{0:T(1024)S(1)}, f32[1024]{0:T(1024)}, u32[]{:S(2)}) copy-start(f32[1024]{0:T(1024)} %param.16) | copy-start | bytes 12292
  55.7 47.2 %copy-start.12 = (s32[64]{0:T(128)S(1)}, s32[64]{0:T(128)}, u32[]{:S(2)}) copy-start(s32[64]{0:T(128)} %param.23) | copy-start | bytes 772
  55.7 39.3 %all-to-all-start = ((bf16[4,272,1024]{2,1,0:T(8,128)(2,1)}), bf16[4,272,1024]{2,1,0:T(8,128)(2,1)S(1)}, u32[]{:S(2)}, u32[]{:S(2)}) async-start(bf16[4,272,1024]{2,1,0:T(8,128)(2,1)} %copy-done.1), calls=%async_computation | async-start | bytes 4456448 | tf_op jit(solution)/shard_map/all_to_all | solution.py:87
  61.7 42.5 %copy-start.10 = (bf16[16,1024]{1,0:T(8,128)(2,1)S(1)}, bf16[16,1024]{1,0:T(8,128)(2,1)}, u32[]{:S(2)}) copy-start(bf16[16,1024]{1,0:T(8,128)(2,1)} %param.24) | copy-start | bytes 98308
  61.7 58.9 %copy-start.6 = (f32[256]{0:T(256)S(1)}, f32[256]{0:T(256)}, u32[]{:S(2)}) copy-start(f32[256]{0:T(256)} %param.22) | copy-start | bytes 3076
  61.7 58.9 %copy-start.7 = (s32[1,4]{1,0:T(1,128)S(1)}, s32[1,4]{1,0:T(1,128)}, u32[]{:S(2)}) copy-start(s32[1,4]{1,0:T(1,128)} %param.18) | copy-start | bytes 52
  61.7 58.9 %copy-start.8 = (s32[1,4]{1,0:T(1,128)S(1)}, s32[1,4]{1,0:T(1,128)}, u32[]{:S(2)}) copy-start(s32[1,4]{1,0:T(1,128)} %param.19) | copy-start | bytes 52
  61.8 14.2 %collective-permute-start.5 = (bf16[48,1024]{1,0:T(8,128)(2,1)S(1)}, bf16[48,1024]{1,0:T(8,128)(2,1)S(1)}, u32[]{:S(2)}, u32[]{:S(2)}) collective-permute-start(bf16[48,1024]{1,0:T(8,128)(2,1)S(1)} %get-tuple-element.29), channel_id=1, source_target_pairs={{0,96},{8,104},{16,112},{24,120},{32,0},{40,8},{48,16},{56,24},{64... | collective-permute-start | bytes 294920 | tf_op jit(solution)/shard_map/ppermute | solution.py:34
  63.8 17.5 %collective-permute-start.4 = (bf16[48,1024]{1,0:T(8,128)(2,1)S(1)}, bf16[48,1024]{1,0:T(8,128)(2,1)S(1)}, u32[]{:S(2)}, u32[]{:S(2)}) collective-permute-start(bf16[48,1024]{1,0:T(8,128)(2,1)S(1)} %get-tuple-element.28), channel_id=1, source_target_pairs={{0,160},{8,168},{16,176},{24,184},{32,192},{40,200},{48,208},{56,2... | collective-permute-start | bytes 294920 | tf_op jit(solution)/shard_map/ppermute | solution.py:34
  76.0 7.2 %collective-permute-start.3 = (bf16[48,1024]{1,0:T(8,128)(2,1)S(1)}, bf16[48,1024]{1,0:T(8,128)(2,1)S(1)}, u32[]{:S(2)}, u32[]{:S(2)}) collective-permute-start(bf16[48,1024]{1,0:T(8,128)(2,1)S(1)} %get-tuple-element.26), channel_id=1, source_target_pairs={{0,128},{8,136},{16,144},{24,152},{32,160},{40,168},{48,176},{56,1... | collective-permute-start | bytes 294920 | tf_op jit(solution)/shard_map/ppermute | solution.py:34
  79.4 15.6 %collective-permute-start.6 = (bf16[48,1024]{1,0:T(8,128)(2,1)S(1)}, bf16[48,1024]{1,0:T(8,128)(2,1)S(1)}, u32[]{:S(2)}, u32[]{:S(2)}) collective-permute-start(bf16[48,1024]{1,0:T(8,128)(2,1)S(1)} %get-tuple-element.27), channel_id=1, source_target_pairs={{0,224},{8,232},{16,240},{24,248},{32,128},{40,136},{48,144},{56,1... | collective-permute-start | bytes 294920 | tf_op jit(solution)/shard_map/ppermute | solution.py:34
  95.1 25.5 %collective-permute-start.7 = (bf16[4,272,1024]{2,1,0:T(8,128)(2,1)S(1)}, bf16[4,272,1024]{2,1,0:T(8,128)(2,1)}, u32[]{:S(2)}, u32[]{:S(2)}) collective-permute-start(bf16[4,272,1024]{2,1,0:T(8,128)(2,1)S(1)} %all-to-all-done.mine_ref), channel_id=1, source_target_pairs={{0,1},{1,0},{2,3},{3,2},{4,5},{5,4},{6,7},{7,6},{8,9},{9,8},{10,11... | collective-permute-start | bytes 6684680 | tf_op jit(solution)/shard_map/ppermute | solution.py:100
  104.2 16.3 %collective-permute-start.8 = (bf16[8,128]{1,0:T(8,128)(2,1)S(1)}, bf16[8,128]{1,0:T(8,128)(2,1)S(1)}, u32[]{:S(2)}, u32[]{:S(2)}) collective-permute-start(bf16[8,128]{1,0:T(8,128)(2,1)S(1)} %bitcast.26), channel_id=1, source_target_pairs={{0,384},{8,392},{16,400},{24,408},{32,416},{40,424},{48,432},{56,4... | collective-permute-start | bytes 6152 | tf_op jit(solution)/shard_map/ppermute | solution.py:34
  120.6 2.2 %copy-start = (bf16[8192,256]{1,0:T(8,128)(2,1)S(1)}, bf16[8192,256]{1,0:T(8,128)(2,1)}, u32[]{:S(2)}) copy-start(bf16[8192,256]{1,0:T(8,128)(2,1)} %all-gather.2.cloned.1.call-done.weight_ref) | copy-start | bytes 12582916
  122.8 10.8 %copy-start.5 = (s32[15,16]{1,0:T(8,128)S(1)}, s32[15,16]{1,0:T(8,128)}, u32[]{:S(2)}) copy-start(s32[15,16]{1,0:T(8,128)} %tables_ref.1) | copy-start | bytes 2884
  122.8 10.8 %copy-start.9 = (s32[15]{0:T(128)S(1)}, s32[15]{0:T(128)}, u32[]{:S(2)}) copy-start(s32[15]{0:T(128)} %lengths_ref.1) | copy-start | bytes 184
  130.2 6.3 %collective-permute-start.9 = (bf16[8,128]{1,0:T(8,128)(2,1)S(1)}, bf16[8,128]{1,0:T(8,128)(2,1)S(1)}, u32[]{:S(2)}, u32[]{:S(2)}) collective-permute-start(bf16[8,128]{1,0:T(8,128)(2,1)S(1)} %get-tuple-element.25), channel_id=1, source_target_pairs={{0,128},{8,136},{16,144},{24,152},{32,160},{40,168},{48,176},{56,1... | collective-permute-start | bytes 6152 | tf_op jit(solution)/shard_map/ppermute | solution.py:34
  133.6 1.5 %copy-start.2 = (bf16[240,16,256]{2,1,0:T(8,128)(2,1)S(1)}, bf16[240,16,256]{2,1,0:T(8,128)(2,1)}, u32[]{:S(2)}) copy-start(bf16[240,16,256]{2,1,0:T(8,128)(2,1)} %pages_ref.1) | copy-start | bytes 5898244
Sparse Core Ops, SparseCore 0:
  10.1 97.4 all-gather.1

commit v4 on v3

--- a/solution.py
+++ b/solution.py
@@ -76,7 +76,7 @@
     )(lax.axis_index("seq")[None], merged_hidden, merger_weight, text_embed, gain[None, :])
 
 
-def summed_images(shares, merger_bias, text, queries):
+def summed_images(shares, merger_bias, text, asked):
     z = lax.axis_index("seq")
     far, other, near, own = shares
     far = hop(far, 0, -1)
@@ -93,12 +93,12 @@
     other = hop(block(1).astype(BF16), 1, 4)
     own = hop((block(0) + merger_bias).astype(BF16), 1, 0)
     near = (wide(block(3)) + wide(far)).astype(BF16)
-    queries = after(queries, near)
+    asked = hop(after(asked, near), -1, 0)
     near = hop(near, 1, -4)
     rows = (wide(own) + wide(other) + wide(near)).astype(BF16)
-    rows, text = lax.optimization_barrier((rows, text))
+    rows, text, asked = lax.optimization_barrier((rows, text, asked))
     others = lax.ppermute(text, "core", [(0, 1), (1, 0)])
-    return rows, text, others, queries
+    return rows, text, others, asked
 
 
 def soft(scores, live):
@@ -109,17 +109,9 @@
 
 def project_kernel(
     length_ref, core_ref, counts_ref, starts_ref, mine_ref, others_ref, image_ref, bias_ref,
-    cos_ref, sin_ref, asked_ref, weight_ref, cache_ref, fresh_ref, held_ref, arrived_ref,
+    cos_ref, sin_ref, asked_ref, weight_ref, cache_ref, fresh_ref,
 ):
-    chunks, depth = held_ref.shape[0], held_ref.shape[1]
-    copies = [
-        pltpu.make_async_copy(
-            weight_ref.at[pl.ds(k * depth, depth), :], held_ref.at[k], arrived_ref.at[k]
-        )
-        for k in range(chunks)
-    ]
-    for copy in copies:
-        copy.start()
+    chunks, depth = 2 * mine_ref.shape[0], mine_ref.shape[2]
     rows = cache_ref.shape[0]
     images = image_ref.shape[0]
     widened = wide(image_ref[...])
@@ -147,15 +139,13 @@
     text_total = jnp.zeros((rows, cache_ref.shape[1]), F32)
     image_total = jnp.zeros((images, cache_ref.shape[1]), F32)
     for row in range(chunks // 2):
-        copies[2 * row].wait()
-        copies[2 * row + 1].wait()
         for ref, side in sides:
             chunk = 2 * row + side
             for first in range(0, depth, 256):
                 part = slice(first, first + 256)
                 columns = pl.ds(pl.multiple_of(chunk * depth + first, 256), 256)
                 gain = wide(ref[row, rows:, part])[:1]
-                weight = held_ref[chunk, part, :]
+                weight = weight_ref[columns, :]
                 normed = wide(ref[row, :rows, part]) * text_scaling * gain
                 text_total = text_total + jnp.dot(
                     normed.astype(BF16), weight, preferred_element_type=F32
@@ -194,7 +184,6 @@
     cosine, sine = jnp.cos(angles), jnp.sin(angles)
     cosine = jnp.concatenate([cosine, cosine], axis=1)
     sine = jnp.concatenate([-sine, sine], axis=1)
-    chunks = 8
     columns = weight.shape[1]
     return pl.pallas_call(
         project_kernel,
@@ -202,12 +191,8 @@
             jax.ShapeDtypeStruct((positions, columns), BF16),
             jax.ShapeDtypeStruct(asked.shape, BF16),
         ),
-        in_specs=[whole(pltpu.SMEM)] * 4 + [whole()] * 7 + [whole(pl.ANY)],
+        in_specs=[whole(pltpu.SMEM)] * 4 + [whole()] * 8,
         out_specs=(whole(), whole()),
-        scratch_shapes=[
-            pltpu.VMEM((chunks, D // chunks, columns), BF16),
-            pltpu.SemaphoreType.DMA((chunks,)),
-        ],
         cost_estimate=SMALL,
         compiler_params=pltpu.CompilerParams(vmem_limit_bytes=VMEM_BYTES),
         name="project",
@@ -289,10 +274,10 @@
 ):
     weight = lax.all_gather(kv_weight, "seq", axis=0, tiled=True)
     *shares, text = merger_shares(merged_hidden, merger_weight, text_embed, prefill_gain)
-    image_rows, text, others, queries = summed_images(shares, merger_bias, text, queries)
+    resident = queries.shape[0] - 1
+    asked = queries[resident:].reshape(-1, HD)
+    image_rows, text, others, asked = summed_images(shares, merger_bias, text, asked)
     image_all = lax.all_gather(image_rows, TP, axis=1, tiled=True)
-    resident = queries.shape[0] - 1
-    asked = hop(queries[resident:].reshape(-1, HD), -1, 0)
     resident_out = attend_resident(queries, cache_pages, page_tables, context_lengths)
     place = lax.axis_index("section") * lax.axis_size("seq") + lax.axis_index("seq")
     length = lax.dynamic_slice_in_dim(prompt_lengths, place, 1, 0)

time: 145 us -> 141 us (0.972)
  waiting for transfers between devices: 40.4 us -> 37.7 us
    ppermute x9, waiting for transfers between devices: 39.7 us -> 37 us  [hop(): return lax.ppermute(value, ('section', 'seq'), pairs)]
where the time goes in v4:
time: 141 us; the launch traced here: 140 us
  starting transfers between devices  53.7 us (38%)
  waiting for transfers between devices  37.7 us (27%)
  between operations  14.4 us (10%)
  blocking collectives  14.2 us (10%)
  Pallas kernels  9.59 us (7%)
  local copies, waits for them, and re-layouts  8.61 us (6%)
  other arithmetic  1.65 us (1%)
    ppermute x9, starting transfers between devices, hop(): return lax.ppermute(value, ('section', 'seq'), pairs)  40.2 us
    ppermute x9, waiting for transfers between devices, hop(): return lax.ppermute(value, ('section', 'seq'), pairs)  37 us
    all_gather x1, blocking collectives, per_device(): image_all = lax.all_gather(image_rows, TP, axis=1, tiled=True)  14.2 us
    ppermute x1, starting transfers between devices, summed_images(): others = lax.ppermute(text, 'core', [(0, 1), (1, 0)])  7.36 us
    unnamed x27, local copies, waits for them, and re-layouts  7.22 us
    pallas_call x1, Pallas kernels, project(): pl.pallas_call(project_kernel, out_shape=(jax.ShapeDtypeStruct((positions...  6.24 us
    all_to_all x1, starting transfers between devices, summed_images(): text = lax.all_to_all(text, 'row', 0, 0, tiled=True)  6.08 us
  transfers between devices with their start and end apart: 12, of which 6 were waited for; matrix products, arithmetic and copies ran while one was open for 3% of the time, Pallas kernels for 2%

profile of v4, /device:TPU:1, one launch (start us, length us, event | category | flops | bytes accessed | tf_op | source)
XLA Modules:
  0.0 139.9 jit_solution(14369332028679099600)
XLA Ops:
  7.2 0.7 all-gather.2.cloned.1.call-update
  7.9 1.3 copy.16.hidden_ref
  9.2 0.7 broadcast_in_dim.36.gain_ref
  9.9 1.1 copy-done.3
  11.0 1.0 copy-done.4
  12.1 2.0 %merger_shares.1 = (bf16[192,1024]{1,0:T(8,128)(2,1)S(1)}, bf16[192,1024]{1,0:T(8,128)(2,1)S(1)}, f32[192,1024]{1,0:T(8,128)S(1)}, f32[192,1024]{1,0:T(8,128)S(1)}, bf16[4,272,1024]{2,1,0:T(8,128)(2,1)S(1)}) custom-call(s32[1]{0:T(128)} %bitcast.3.place_ref, bf16[768,320]{1,0:T(8,128)(2,1)S(1)} %copy.16.hidden_ref, bf16[320,1024]{1,0:T(8,128)(2,1)S(1)} %copy-done.3, ...), custom_call_target="tpu_custom_call" | custom-call | flops 1024 | bytes 1024 | tf_op jit(solution)/shard_map/merger_shares/pallas_call | solution.py:68
  14.1 11.9 %collective-permute-start.1 = (bf16[192,1024]{1,0:T(8,128)(2,1)S(1)}, bf16[192,1024]{1,0:T(8,128)(2,1)S(1)}, u32[]{:S(2)}, u32[]{:S(2)}) collective-permute-start(bf16[192,1024]{1,0:T(8,128)(2,1)S(1)} %get-tuple-element.18), channel_id=1, source_target_pairs={{0,120},{8,0},{16,8},{24,16},{32,24},{40,32},{48,40},{56,48},{64,5... | collective-permute-start | bytes 1179656 | tf_op jit(solution)/shard_map/ppermute | solution.py:34
  26.0 1.9 %collective-permute-start = (bf16[192,1024]{1,0:T(8,128)(2,1)S(1)}, bf16[192,1024]{1,0:T(8,128)(2,1)S(1)}, u32[]{:S(2)}, u32[]{:S(2)}) collective-permute-start(bf16[192,1024]{1,0:T(8,128)(2,1)S(1)} %get-tuple-element.16), channel_id=1, source_target_pairs={{0,8},{8,16},{16,24},{24,32},{32,40},{40,48},{48,56},{56,64},{64,7... | collective-permute-start | bytes 1179656 | tf_op jit(solution)/shard_map/ppermute | solution.py:34
  28.0 7.3 %collective-permute-done.1 = bf16[192,1024]{1,0:T(8,128)(2,1)S(1)} collective-permute-done((bf16[192,1024]{1,0:T(8,128)(2,1)S(1)}, bf16[192,1024]{1,0:T(8,128)(2,1)S(1)}, u32[]{:S(2)}, u32[]{:S(2)}) %collective-permute-start.1) | collective-permute-done | bytes 393248 | tf_op jit(solution)/shard_map/ppermute | solution.py:34
  35.4 5.4 %collective-permute-start.2 = (bf16[192,1024]{1,0:T(8,128)(2,1)S(1)}, bf16[192,1024]{1,0:T(8,128)(2,1)S(1)}, u32[]{:S(2)}, u32[]{:S(2)}) collective-permute-start(bf16[192,1024]{1,0:T(8,128)(2,1)S(1)} %add_convert_fusion), channel_id=1, source_target_pairs={{0,120},{8,0},{16,8},{24,16},{32,24},{40,32},{48,40},{56,48},{64,5... | collective-permute-start | bytes 1179656 | tf_op jit(solution)/shard_map/ppermute | solution.py:34
  40.8 0.4 collective-permute-done
  41.2 14.4 %collective-permute-done.2 = bf16[192,1024]{1,0:T(8,128)(2,1)S(1)} collective-permute-done((bf16[192,1024]{1,0:T(8,128)(2,1)S(1)}, bf16[192,1024]{1,0:T(8,128)(2,1)S(1)}, u32[]{:S(2)}, u32[]{:S(2)}) %collective-permute-start.2) | collective-permute-done | bytes 393248 | tf_op jit(solution)/shard_map/ppermute | solution.py:34
  55.5 0.1 convert_add_fusion
  55.7 6.1 %all-to-all-start = ((bf16[4,272,1024]{2,1,0:T(8,128)(2,1)}), bf16[4,272,1024]{2,1,0:T(8,128)(2,1)S(1)}, u32[]{:S(2)}, u32[]{:S(2)}) async-start(bf16[4,272,1024]{2,1,0:T(8,128)(2,1)} %copy-done.1), calls=%async_computation | async-start | bytes 4456448 | tf_op jit(solution)/shard_map/all_to_all | solution.py:87
  61.9 2.0 %collective-permute-start.5 = (bf16[48,1024]{1,0:T(8,128)(2,1)S(1)}, bf16[48,1024]{1,0:T(8,128)(2,1)S(1)}, u32[]{:S(2)}, u32[]{:S(2)}) collective-permute-start(bf16[48,1024]{1,0:T(8,128)(2,1)S(1)} %get-tuple-element.31), channel_id=1, source_target_pairs={{0,96},{8,104},{16,112},{24,120},{32,0},{40,8},{48,16},{56,24},{64... | collective-permute-start | bytes 294920 | tf_op jit(solution)/shard_map/ppermute | solution.py:34
  64.0 8.2 %collective-permute-start.4 = (bf16[48,1024]{1,0:T(8,128)(2,1)S(1)}, bf16[48,1024]{1,0:T(8,128)(2,1)S(1)}, u32[]{:S(2)}, u32[]{:S(2)}) collective-permute-start(bf16[48,1024]{1,0:T(8,128)(2,1)S(1)} %get-tuple-element.30), channel_id=1, source_target_pairs={{0,160},{8,168},{16,176},{24,184},{32,192},{40,200},{48,208},{56,2... | collective-permute-start | bytes 294920 | tf_op jit(solution)/shard_map/ppermute | solution.py:34
  72.2 3.9 %collective-permute-done.5 = bf16[48,1024]{1,0:T(8,128)(2,1)S(1)} collective-permute-done((bf16[48,1024]{1,0:T(8,128)(2,1)S(1)}, bf16[48,1024]{1,0:T(8,128)(2,1)S(1)}, u32[]{:S(2)}, u32[]{:S(2)}) %collective-permute-start.5) | collective-permute-done | bytes 98336 | tf_op jit(solution)/shard_map/ppermute | solution.py:34
  76.1 3.4 %collective-permute-start.3 = (bf16[48,1024]{1,0:T(8,128)(2,1)S(1)}, bf16[48,1024]{1,0:T(8,128)(2,1)S(1)}, u32[]{:S(2)}, u32[]{:S(2)}) collective-permute-start(bf16[48,1024]{1,0:T(8,128)(2,1)S(1)} %get-tuple-element.28), channel_id=1, source_target_pairs={{0,128},{8,136},{16,144},{24,152},{32,160},{40,168},{48,176},{56,1... | collective-permute-start | bytes 294920 | tf_op jit(solution)/shard_map/ppermute | solution.py:34
  79.5 1.9 %collective-permute-start.6 = (bf16[48,1024]{1,0:T(8,128)(2,1)S(1)}, bf16[48,1024]{1,0:T(8,128)(2,1)S(1)}, u32[]{:S(2)}, u32[]{:S(2)}) collective-permute-start(bf16[48,1024]{1,0:T(8,128)(2,1)S(1)} %get-tuple-element.29), channel_id=1, source_target_pairs={{0,224},{8,232},{16,240},{24,248},{32,128},{40,136},{48,144},{56,1... | collective-permute-start | bytes 294920 | tf_op jit(solution)/shard_map/ppermute | solution.py:34
  81.5 3.3 %collective-permute-start.7 = (bf16[8,128]{1,0:T(8,128)(2,1)S(1)}, bf16[8,128]{1,0:T(8,128)(2,1)S(1)}, u32[]{:S(2)}, u32[]{:S(2)}) collective-permute-start(bf16[8,128]{1,0:T(8,128)(2,1)S(1)} %bitcast.25), channel_id=1, source_target_pairs={{0,384},{8,392},{16,400},{24,408},{32,416},{40,424},{48,432},{56,4... | collective-permute-start | bytes 6152 | tf_op jit(solution)/shard_map/ppermute | solution.py:34
  84.8 10.6 %collective-permute-done.6 = bf16[48,1024]{1,0:T(8,128)(2,1)S(1)} collective-permute-done((bf16[48,1024]{1,0:T(8,128)(2,1)S(1)}, bf16[48,1024]{1,0:T(8,128)(2,1)S(1)}, u32[]{:S(2)}, u32[]{:S(2)}) %collective-permute-start.6) | collective-permute-done | bytes 98336 | tf_op jit(solution)/shard_map/ppermute | solution.py:34
  95.5 7.4 %collective-permute-start.8 = (bf16[4,272,1024]{2,1,0:T(8,128)(2,1)S(1)}, bf16[4,272,1024]{2,1,0:T(8,128)(2,1)}, u32[]{:S(2)}, u32[]{:S(2)}) collective-permute-start(bf16[4,272,1024]{2,1,0:T(8,128)(2,1)S(1)} %all-to-all-done.mine_ref), channel_id=1, source_target_pairs={{0,1},{1,0},{2,3},{3,2},{4,5},{5,4},{6,7},{7,6},{8,9},{9,8},{10,11... | collective-permute-start | bytes 6684680 | tf_op jit(solution)/shard_map/ppermute | solution.py:100
  102.9 0.6 dynamic_slice.16.length_ref
  103.5 0.5 fusion.6
  104.2 14.2 %all_gather.6.image_ref = bf16[48,8192]{1,0:T(8,128)(2,1)S(1)} all-gather(bf16[48,1024]{1,0:T(8,128)(2,1)S(1)} %add_convert_fusion.1), channel_id=1, replica_groups=mesh['section'=4,'seq'=16,'row'=4,'core'=2] {'row','core'}, dimensions={1}, use_global_device_ids=true | all-gather | bytes 884736 | tf_op jit(solution)/shard_map/all_gather | solution.py:280
  118.4 2.2 %copy-done = bf16[8192,256]{1,0:T(8,128)(2,1)S(1)} copy-done((bf16[8192,256]{1,0:T(8,128)(2,1)S(1)}, bf16[8192,256]{1,0:T(8,128)(2,1)}, u32[]{:S(2)}) %copy-start) | copy-done | bytes 4194328
  120.6 6.2 %project.1 = (bf16[256,256]{1,0:T(8,128)(2,1)}, bf16[8,128]{1,0:T(8,128)(2,1)S(1)}) custom-call(s32[1]{0:T(128)} %dynamic_slice.16.length_ref, s32[1]{0:T(128)} %bitcast.core_ref, s32[4]{0:T(128)S(1)} %bitcast.21, s32[4]{0:T(128)S(1)} %bitcast.22, bf16[4,272,1024]{2,1,0:T(8,128)(2,1)S(1)} %all-to-all-done.mine_ref, ...), custom_call_target="tpu_custom_call" | custom-call | flops 1024 | bytes 1024 | tf_op jit(solution)/shard_map/project/pallas_call | solution.py:188
  126.8 2.1 %collective-permute-start.9 = (bf16[8,128]{1,0:T(8,128)(2,1)S(1)}, bf16[8,128]{1,0:T(8,128)(2,1)S(1)}, u32[]{:S(2)}, u32[]{:S(2)}) collective-permute-start(bf16[8,128]{1,0:T(8,128)(2,1)S(1)} %get-tuple-element.27), channel_id=1, source_target_pairs={{0,128},{8,136},{16,144},{24,152},{32,160},{40,168},{48,176},{56,1... | collective-permute-start | bytes 6152 | tf_op jit(solution)/shard_map/ppermute | solution.py:34
  129.0 1.5 %copy-done.2 = bf16[240,16,256]{2,1,0:T(8,128)(2,1)S(1)} copy-done((bf16[240,16,256]{2,1,0:T(8,128)(2,1)S(1)}, bf16[240,16,256]{2,1,0:T(8,128)(2,1)}, u32[]{:S(2)}) %copy-start.2) | copy-done | bytes 1966104
  130.5 1.3 resident.1
  131.9 0.4 collective-permute-done.9
  132.3 0.7 broadcast_select_fusion
  (39 shorter events, 0.5 us)
Async XLA Ops:
  7.2 111.2 %all-gather.2.cloned.1.call-start = ((), (), s32[]{:S(2)}) async-start(), calls=%async_computation.1 | async-start | bytes 4456448 | tf_op jit(solution)/shard_map/all_gather | solution.py:275
  9.9 1.1 copy-start.3
  11.0 1.0 copy-start.4
  14.1 41.6 %copy-start.1 = (bf16[4,272,1024]{2,1,0:T(8,128)(2,1)}, bf16[4,272,1024]{2,1,0:T(8,128)(2,1)S(1)}, u32[]{:S(2)}) copy-start(bf16[4,272,1024]{2,1,0:T(8,128)(2,1)S(1)} %get-tuple-element.21) | copy-start | bytes 6684676
  14.1 21.2 %collective-permute-start.1 = (bf16[192,1024]{1,0:T(8,128)(2,1)S(1)}, bf16[192,1024]{1,0:T(8,128)(2,1)S(1)}, u32[]{:S(2)}, u32[]{:S(2)}) collective-permute-start(bf16[192,1024]{1,0:T(8,128)(2,1)S(1)} %get-tuple-element.18), channel_id=1, source_target_pairs={{0,120},{8,0},{16,8},{24,16},{32,24},{40,32},{48,40},{56,48},{64,5... | collective-permute-start | bytes 1179656 | tf_op jit(solution)/shard_map/ppermute | solution.py:34
  26.0 15.1 %collective-permute-start = (bf16[192,1024]{1,0:T(8,128)(2,1)S(1)}, bf16[192,1024]{1,0:T(8,128)(2,1)S(1)}, u32[]{:S(2)}, u32[]{:S(2)}) collective-permute-start(bf16[192,1024]{1,0:T(8,128)(2,1)S(1)} %get-tuple-element.16), channel_id=1, source_target_pairs={{0,8},{8,16},{16,24},{24,32},{32,40},{40,48},{48,56},{56,64},{64,7... | collective-permute-start | bytes 1179656 | tf_op jit(solution)/shard_map/ppermute | solution.py:34
  35.4 20.1 %collective-permute-start.2 = (bf16[192,1024]{1,0:T(8,128)(2,1)S(1)}, bf16[192,1024]{1,0:T(8,128)(2,1)S(1)}, u32[]{:S(2)}, u32[]{:S(2)}) collective-permute-start(bf16[192,1024]{1,0:T(8,128)(2,1)S(1)} %add_convert_fusion), channel_id=1, source_target_pairs={{0,120},{8,0},{16,8},{24,16},{32,24},{40,32},{48,40},{56,48},{64,5... | collective-permute-start | bytes 1179656 | tf_op jit(solution)/shard_map/ppermute | solution.py:34
  55.7 20.4 %copy-start.11 = (f32[1024]{0:T(1024)S(1)}, f32[1024]{0:T(1024)}, u32[]{:S(2)}) copy-start(f32[1024]{0:T(1024)} %param.16) | copy-start | bytes 12292
  55.7 25.7 %copy-start.10 = (bf16[16,1024]{1,0:T(8,128)(2,1)S(1)}, bf16[16,1024]{1,0:T(8,128)(2,1)}, u32[]{:S(2)}) copy-start(bf16[16,1024]{1,0:T(8,128)(2,1)} %param.24) | copy-start | bytes 98308
  55.7 47.2 %copy-start.12 = (s32[64]{0:T(128)S(1)}, s32[64]{0:T(128)}, u32[]{:S(2)}) copy-start(s32[64]{0:T(128)} %param.23) | copy-start | bytes 772
  55.7 39.8 %all-to-all-start = ((bf16[4,272,1024]{2,1,0:T(8,128)(2,1)}), bf16[4,272,1024]{2,1,0:T(8,128)(2,1)S(1)}, u32[]{:S(2)}, u32[]{:S(2)}) async-start(bf16[4,272,1024]{2,1,0:T(8,128)(2,1)} %copy-done.1), calls=%async_computation | async-start | bytes 4456448 | tf_op jit(solution)/shard_map/all_to_all | solution.py:87
  61.8 56.5 %copy-start.6 = (f32[256]{0:T(256)S(1)}, f32[256]{0:T(256)}, u32[]{:S(2)}) copy-start(f32[256]{0:T(256)} %param.22) | copy-start | bytes 3076
  61.8 56.5 %copy-start.7 = (s32[1,4]{1,0:T(1,128)S(1)}, s32[1,4]{1,0:T(1,128)}, u32[]{:S(2)}) copy-start(s32[1,4]{1,0:T(1,128)} %param.18) | copy-start | bytes 52
  61.8 56.5 %copy-start.8 = (s32[1,4]{1,0:T(1,128)S(1)}, s32[1,4]{1,0:T(1,128)}, u32[]{:S(2)}) copy-start(s32[1,4]{1,0:T(1,128)} %param.19) | copy-start | bytes 52
  61.9 14.1 %collective-permute-start.5 = (bf16[48,1024]{1,0:T(8,128)(2,1)S(1)}, bf16[48,1024]{1,0:T(8,128)(2,1)S(1)}, u32[]{:S(2)}, u32[]{:S(2)}) collective-permute-start(bf16[48,1024]{1,0:T(8,128)(2,1)S(1)} %get-tuple-element.31), channel_id=1, source_target_pairs={{0,96},{8,104},{16,112},{24,120},{32,0},{40,8},{48,16},{56,24},{64... | collective-permute-start | bytes 294920 | tf_op jit(solution)/shard_map/ppermute | solution.py:34
  64.0 20.8 %collective-permute-start.4 = (bf16[48,1024]{1,0:T(8,128)(2,1)S(1)}, bf16[48,1024]{1,0:T(8,128)(2,1)S(1)}, u32[]{:S(2)}, u32[]{:S(2)}) collective-permute-start(bf16[48,1024]{1,0:T(8,128)(2,1)S(1)} %get-tuple-element.30), channel_id=1, source_target_pairs={{0,160},{8,168},{16,176},{24,184},{32,192},{40,200},{48,208},{56,2... | collective-permute-start | bytes 294920 | tf_op jit(solution)/shard_map/ppermute | solution.py:34
  76.1 8.7 %collective-permute-start.3 = (bf16[48,1024]{1,0:T(8,128)(2,1)S(1)}, bf16[48,1024]{1,0:T(8,128)(2,1)S(1)}, u32[]{:S(2)}, u32[]{:S(2)}) collective-permute-start(bf16[48,1024]{1,0:T(8,128)(2,1)S(1)} %get-tuple-element.28), channel_id=1, source_target_pairs={{0,128},{8,136},{16,144},{24,152},{32,160},{40,168},{48,176},{56,1... | collective-permute-start | bytes 294920 | tf_op jit(solution)/shard_map/ppermute | solution.py:34
  79.5 15.9 %collective-permute-start.6 = (bf16[48,1024]{1,0:T(8,128)(2,1)S(1)}, bf16[48,1024]{1,0:T(8,128)(2,1)S(1)}, u32[]{:S(2)}, u32[]{:S(2)}) collective-permute-start(bf16[48,1024]{1,0:T(8,128)(2,1)S(1)} %get-tuple-element.29), channel_id=1, source_target_pairs={{0,224},{8,232},{16,240},{24,248},{32,128},{40,136},{48,144},{56,1... | collective-permute-start | bytes 294920 | tf_op jit(solution)/shard_map/ppermute | solution.py:34
  81.5 14.0 %collective-permute-start.7 = (bf16[8,128]{1,0:T(8,128)(2,1)S(1)}, bf16[8,128]{1,0:T(8,128)(2,1)S(1)}, u32[]{:S(2)}, u32[]{:S(2)}) collective-permute-start(bf16[8,128]{1,0:T(8,128)(2,1)S(1)} %bitcast.25), channel_id=1, source_target_pairs={{0,384},{8,392},{16,400},{24,408},{32,416},{40,424},{48,432},{56,4... | collective-permute-start | bytes 6152 | tf_op jit(solution)/shard_map/ppermute | solution.py:34
  95.5 22.8 %collective-permute-start.8 = (bf16[4,272,1024]{2,1,0:T(8,128)(2,1)S(1)}, bf16[4,272,1024]{2,1,0:T(8,128)(2,1)}, u32[]{:S(2)}, u32[]{:S(2)}) collective-permute-start(bf16[4,272,1024]{2,1,0:T(8,128)(2,1)S(1)} %all-to-all-done.mine_ref), channel_id=1, source_target_pairs={{0,1},{1,0},{2,3},{3,2},{4,5},{5,4},{6,7},{7,6},{8,9},{9,8},{10,11... | collective-permute-start | bytes 6684680 | tf_op jit(solution)/shard_map/ppermute | solution.py:100
  118.4 2.2 %copy-start = (bf16[8192,256]{1,0:T(8,128)(2,1)S(1)}, bf16[8192,256]{1,0:T(8,128)(2,1)}, u32[]{:S(2)}) copy-start(bf16[8192,256]{1,0:T(8,128)(2,1)} %all-gather.2.cloned.1.call-done.weight_ref) | copy-start | bytes 12582916
  120.6 8.4 %copy-start.5 = (s32[15,16]{1,0:T(8,128)S(1)}, s32[15,16]{1,0:T(8,128)}, u32[]{:S(2)}) copy-start(s32[15,16]{1,0:T(8,128)} %tables_ref.1) | copy-start | bytes 2884
  120.6 8.4 %copy-start.9 = (s32[15]{0:T(128)S(1)}, s32[15]{0:T(128)}, u32[]{:S(2)}) copy-start(s32[15]{0:T(128)} %lengths_ref.1) | copy-start | bytes 184
  126.8 5.5 %collective-permute-start.9 = (bf16[8,128]{1,0:T(8,128)(2,1)S(1)}, bf16[8,128]{1,0:T(8,128)(2,1)S(1)}, u32[]{:S(2)}, u32[]{:S(2)}) collective-permute-start(bf16[8,128]{1,0:T(8,128)(2,1)S(1)} %get-tuple-element.27), channel_id=1, source_target_pairs={{0,128},{8,136},{16,144},{24,152},{32,160},{40,168},{48,176},{56,1... | collective-permute-start | bytes 6152 | tf_op jit(solution)/shard_map/ppermute | solution.py:34
  129.0 1.5 %copy-start.2 = (bf16[240,16,256]{2,1,0:T(8,128)(2,1)S(1)}, bf16[240,16,256]{2,1,0:T(8,128)(2,1)}, u32[]{:S(2)}) copy-start(bf16[240,16,256]{2,1,0:T(8,128)(2,1)} %pages_ref.1) | copy-start | bytes 5898244
Sparse Core Ops, SparseCore 0:
  10.1 97.6 all-gather.1
